TPU v7x, 512 devices: a whole 4x8x8 slice. The times are simulated.
512 devices in a mesh: sector: 8 (over y), term: 64 (over x, z, core).
Axes of the slice: x: 4, y: 8, z: 8, core: 2. Of those that a mesh axis runs over, the one named last changes fastest.
Arguments:
- wave_in: bfloat16 [16, 1024, 256], P('sector'), may hold values from -6 to 6
- left_env: bfloat16 [16, 192, 1024, 256], P('sector', 'term'), may hold values from -0.1875 to 0.1875
- right_env: bfloat16 [16, 192, 256, 64], P('sector', 'term'), may hold values from -0.375 to 0.375
- shift_map: int32 [48, 16], replicated, may hold values from 0 to 15
- live_rows: int32 [16], replicated, may hold values from 512 to 1024
Outputs:
- isometry: bfloat16 [16, 1024, 256], P('sector', 'term')
- env_next: bfloat16 [16, 192, 256, 64], P('sector', 'term')
All inputs are finite; a program needn't handle non-finite values.
Results may differ from a plain program's by a relative error of at most 0.014.
Values may be sent and summed in bfloat16 or wider, within the bound.
A program may use at most 64 MiB of HBM per device.

v0:
```python
import math

import jax
import jax.numpy as jnp
from jax import lax
from jax.sharding import Mesh
from jax.sharding import PartitionSpec as P

STEPS = 8
TERM = ("term_0", "term_1", "term_2")


step_size = 0.15
epsilon = 1e-06
highest = lax.Precision.HIGHEST


def from_partner(block, axis, bit):
    count = lax.axis_size(axis)
    route = []
    for low in range(count):
        high = low | 1 << bit
        if high != low and high < count:
            route += [(low, high), (high, low)]
    return lax.ppermute(block, axis, route)


def in_order(pieces, dim):
    lengths = list(pieces.shape[1:])
    lengths[dim] *= pieces.shape[0]
    return jnp.moveaxis(pieces, 0, dim).reshape(lengths)


def copy_for_each(shard, axis):
    copies = jnp.broadcast_to(shard, (lax.axis_size(axis), *shard.shape))
    return lax.all_to_all(copies, axis, split_axis=0, concat_axis=0, tiled=True)


def collect(shard, axis, dim):
    return in_order(copy_for_each(shard, axis), dim)


def filled_up(lines, peers):
    spare = -len(lines) % peers
    return jnp.pad(lines, [(0, spare)] + [(0, 0)] * (lines.ndim - 1))


def gather_axes(shard, axes, dim):
    far, near = axes
    pieces = copy_for_each(copy_for_each(shard, far), near)
    return in_order(pieces.swapaxes(0, 1).reshape(-1, *shard.shape), dim)


def split_up(shard, dim, peers):
    lengths = shard.shape
    pieces = shard.reshape(*lengths[:dim], peers, lengths[dim] // peers, *lengths[dim + 1 :])
    return jnp.moveaxis(pieces, dim, 0)


def summed_on_arrival(shard, axis, dim):
    peers = lax.axis_size(axis)
    pieces = lax.all_to_all(split_up(shard, dim, peers), axis, 0, 0, tiled=True)
    return jnp.sum(pieces.astype(jnp.float32), axis=0)


def sum_by_axis(shard, axes, dim):
    far, near = axes
    own = summed_on_arrival(split_up(shard, dim, lax.axis_size(far)), near, dim + 1)
    return jnp.sum(
        lax.all_to_all(own.astype(jnp.bfloat16), far, 0, 0, tiled=True).astype(jnp.float32), axis=0
    )


def sum_by_parts(shard, axes):
    lines = shard.reshape(-1, shard.shape[-1])
    padded = filled_up(lines, lax.axis_size(axes[0]) * lax.axis_size(axes[1]))
    whole = gather_axes(sum_by_axis(padded, axes, 0).astype(jnp.bfloat16), axes, 0)
    return lax.slice_in_dim(whole, 0, len(lines)).reshape(shard.shape).astype(jnp.float32)


def body(wave_in, left_env, right_env, shift_map, live_rows):
    sec_dev, width_left, width_right = wave_in.shape
    pair_dev = left_env.shape[1]
    slices = width_left // left_env.shape[3]
    left_part = width_left // slices
    levels = slices.bit_length() - 1
    term_pos = lax.axis_index(TERM)
    slice_pos = term_pos % slices
    group_pos = term_pos // slices
    first_sector = lax.axis_index("sector") * sec_dev
    blocks = right_env[:, :, :, None, :]
    for bit_level in range(levels):
        partner = from_partner(blocks, TERM, bit_level)
        upper_half = slice_pos // 2**bit_level % 2 == 1
        blocks = jnp.concatenate(
            [jnp.where(upper_half, partner, blocks), jnp.where(upper_half, blocks, partner)], axis=3
        )
    right_complete = blocks.reshape(sec_dev, pair_dev, width_right, width_right)
    terms_here = lax.dynamic_slice_in_dim(shift_map, group_pos * pair_dev, pair_dev, 0)
    sources = lax.dynamic_slice_in_dim(terms_here, first_sector, sec_dev, 1).T
    limits = lax.dynamic_slice_in_dim(live_rows, first_sector, sec_dev, 0)
    mine_rows = lax.dynamic_slice_in_dim(wave_in, slice_pos * left_part, left_part, 1)
    every_rows = collect(mine_rows, "sector", 0)
    selected_block = every_rows[sources]
    operator_applied = jnp.einsum(
        "spab,spbc->spac", selected_block, right_complete, preferred_element_type=jnp.float32
    ).astype(jnp.bfloat16)
    row_share = width_left // lax.axis_size(TERM)
    term_total = jnp.einsum(
        "spia,spac->sic", left_env, operator_applied, preferred_element_type=jnp.float32
    )
    sigma_block_sum = sum_by_parts(
        term_total.astype(jnp.bfloat16), (("term_0", "term_1"), "term_2")
    )
    row_total = sigma_block_sum.shape[1]
    own_rows = wave_in.astype(jnp.float32)
    row_index = jnp.arange(row_total, dtype=jnp.int32)
    live_mask = row_index[None, :, None] < limits[:, None, None]
    updated = jnp.where(live_mask, own_rows - step_size * sigma_block_sum, 0.0)
    gram_sum = jnp.einsum("sia,sib->sab", updated, updated, precision=highest)
    trace_sum = jnp.trace(gram_sum, axis1=1, axis2=2) + epsilon
    identity = jnp.eye(width_right, dtype=jnp.float32)
    root_part = gram_sum / trace_sum[:, None, None]
    inverse_part = jnp.broadcast_to(identity, root_part.shape)
    for ns_step in range(STEPS):
        ns_factor = 1.5 * identity - 0.5 * jnp.einsum(
            "sab,sbc->sac", inverse_part, root_part, precision=highest
        )
        root_part = jnp.einsum("sab,sbc->sac", root_part, ns_factor, precision=highest)
        inverse_part = jnp.einsum("sab,sbc->sac", ns_factor, inverse_part, precision=highest)
    result = (
        jnp.einsum("sia,sab->sib", updated, inverse_part, precision=highest)
        * jnp.sqrt(width_left / trace_sum)[:, None, None]
    )
    wave_rows = result.astype(jnp.bfloat16)
    wave_out = lax.dynamic_slice_in_dim(wave_rows, term_pos * row_share, row_share, 1)
    source_rows = lax.dynamic_slice_in_dim(wave_rows, slice_pos * left_part, left_part, 1)
    every_source = collect(source_rows, "sector", 0)
    picked_wave = every_source[sources]
    projected_wave = jnp.einsum(
        "sia,spib->spab", wave_rows, left_env, preferred_element_type=jnp.float32
    ).astype(jnp.bfloat16)
    partial_value = jnp.einsum(
        "spab,spbc->spac", projected_wave, picked_wave, preferred_element_type=jnp.float32
    )
    blocks = partial_value.reshape(sec_dev, pair_dev, width_right, slices, width_right // slices)
    for bit_level in reversed(range(levels)):
        half_count = blocks.shape[3] // 2
        upper_half = slice_pos // 2**bit_level % 2 == 1
        low_half = blocks[:, :, :, :half_count]
        high_half = blocks[:, :, :, half_count:]
        kept_half = jnp.where(upper_half, high_half, low_half)
        sent_half = jnp.where(upper_half, low_half, high_half)
        blocks = kept_half + from_partner(sent_half.astype(jnp.bfloat16), TERM, bit_level).astype(
            sent_half.dtype
        )
    environment_block = (blocks[:, :, :, 0] / math.sqrt(width_left)).astype(jnp.bfloat16)
    return (wave_out, environment_block)


def solution(mesh):
    split = Mesh(
        mesh.devices.reshape(mesh.shape["sector"], 4, 8, 2),
        ("sector", "term_0", "term_1", "term_2"),
    )
    return jax.shard_map(
        body,
        mesh=split,
        in_specs=(
            P("sector", None, None),
            P("sector", TERM, None, None),
            P("sector", TERM, None, None),
            P(),
            P(),
        ),
        out_specs=(P("sector", TERM, None), P("sector", TERM, None, None)),
        check_vma=False,
    )
```

profile of v0, /device:TPU:1, one launch (start us, length us, event | category | flops | bytes accessed | tf_op | source)
XLA Modules:
  0.0 250.3 jit_solution(1117239266160874001)
XLA Ops:
  0.7 1.1 constant_dynamic-slice_fusion.2
  1.8 1.5 broadcast_in_dim.58
  3.3 7.8 %all-to-all-start = ((bf16[8,2,256,256]{3,2,1,0:T(8,128)(2,1)}), bf16[8,2,256,256]{3,2,1,0:T(8,128)(2,1)}, u32[]{:S(2)}, u32[]{:S(2)}) async-start(bf16[8,2,256,256]{3,2,1,0:T(8,128)(2,1)} %broadcast_in_dim.58), calls=%async_computation | async-start | bytes 4194304 | tf_op jit(solution)/shard_map/all_to_all | solution.py:36
  11.1 5.5 %collective-permute-start = (bf16[2,3,256,1,64]{2,4,3,1,0:T(8,128)(2,1)S(1)}, bf16[2,3,256,1,64]{2,4,3,1,0:T(8,128)(2,1)}, u32[]{:S(2)}, u32[]{:S(2)}) collective-permute-start(bf16[2,3,256,1,64]{2,4,3,1,0:T(8,128)(2,1)S(1)} %bitcast.93), channel_id=1, source_target_pairs={{0,1},{1,0},{2,3},{3,2},{4,5},{5,4},{6,7},{7,6},{8,9},{9,8},{10,11... | collective-permute-start | bytes 589832 | tf_op jit(solution)/shard_map/ppermute | solution.py:25
  16.7 1.2 collective-permute-done
  17.8 1.1 broadcast_select_fusion.3
  18.9 0.8 pad_maximum_fusion.1
  19.7 1.9 collective-permute-start.1
  21.6 0.8 compare_select_fusion
  22.5 9.7 %collective-permute-done.1 = bf16[2,3,256,2,64]{2,4,3,1,0:T(8,128)(2,1)} collective-permute-done((bf16[2,3,256,2,64]{2,4,3,1,0:T(8,128)(2,1)}, bf16[2,3,256,2,64]{2,4,3,1,0:T(8,128)(2,1)}, u32[]{:S(2)}, u32[]{:S(2)}) %collective-permute-start.1) | collective-permute-done | bytes 393248 | tf_op jit(solution)/shard_map/ppermute | solution.py:25
  32.2 1.1 broadcast_select_fusion.1
  33.2 0.9 pad_maximum_fusion
  34.2 25.5 %all-to-all-done = bf16[8,2,256,256]{3,2,1,0:T(8,128)(2,1)} async-done(((bf16[8,2,256,256]{3,2,1,0:T(8,128)(2,1)}), bf16[8,2,256,256]{3,2,1,0:T(8,128)(2,1)}, u32[]{:S(2)}, u32[]{:S(2)}) %all-to-all-start) | async-done | bytes 2097184 | tf_op jit(solution)/shard_map/all_to_all | solution.py:36
  59.7 3.1 %gather_fusion = bf16[6,256,256]{2,1,0:T(8,128)(2,1)} fusion(bf16[16,256,256]{2,1,0:T(8,128)(2,1)} %bitcast, s32[1024]{0:T(1024)S(1)} %pad_clamp_fusion), kind=kCustom, calls=%fused_computation | custom fusion | bytes 1572888 | tf_op jit(solution)/shard_map/gather | solution.py:104
  62.8 3.7 %fusion = bf16[2,1024,256]{1,2,0:T(8,128)(2,1)} fusion(bf16[2,3,1024,256]{3,2,1,0:T(8,128)(2,1)S(1)} %copy-done, bf16[2,3,256,256]{3,2,1,0:T(8,128)(2,1)} %bitcast.92, bf16[2,3,256,256]{2,3,1,0:T(8,128)(2,1)} %bitcast.91), kind=kOutput, calls=%fused_computation.8 | convolution fusion | flops 1007550464 | bytes 5767168 | tf_op jit(solution)/shard_map/spia,spac->sic/dot_general | solution.py:109
  66.5 2.3 copy.30
  68.8 1.3 copy.31
  70.1 8.6 %all_to_all.30 = bf16[2,32,32,256]{3,2,1,0:T(8,128)(2,1)} all-to-all(bf16[2,32,32,256]{3,2,1,0:T(8,128)(2,1)S(1)} %copy.31), channel_id=1, replica_groups=mesh['sector'=8,'term_0'=4,'term_1'=8,'term_2'=2] {'term_2'}, dimensions={0} | all-to-all | bytes 2097152 | tf_op jit(solution)/shard_map/all_to_all | solution.py:62
  78.7 2.4 reduce_sum.34
  81.1 27.1 %all_to_all.31 = bf16[32,32,256]{2,1,0:T(8,128)(2,1)} all-to-all(bf16[32,32,256]{2,1,0:T(8,128)(2,1)} %reduce_sum.34), channel_id=1, replica_groups=mesh['sector'=8,'term_0'=4,'term_1'=8,'term_2'=2] {'term_0','term_1'}, dimensions={0} | all-to-all | bytes 1048576 | tf_op jit(solution)/shard_map/all_to_all | solution.py:70
  108.3 1.1 reduce_sum.35
  109.4 0.8 broadcast_in_dim.61
  110.3 8.3 %all-to-all-start.3 = ((bf16[32,32,256]{2,1,0:T(8,128)(2,1)}), bf16[32,32,256]{2,1,0:T(8,128)(2,1)}, u32[]{:S(2)}, u32[]{:S(2)}) async-start(bf16[32,32,256]{2,1,0:T(8,128)(2,1)} %broadcast_in_dim.61), calls=%async_computation.3 | async-start | bytes 1048576 | tf_op jit(solution)/shard_map/all_to_all | solution.py:36
  118.7 0.7 fusion.22
  119.5 13.1 %all-to-all-done.3 = bf16[32,32,256]{2,1,0:T(8,128)(2,1)} async-done(((bf16[32,32,256]{2,1,0:T(8,128)(2,1)}), bf16[32,32,256]{2,1,0:T(8,128)(2,1)}, u32[]{:S(2)}, u32[]{:S(2)}) %all-to-all-start.3) | async-done | bytes 524320 | tf_op jit(solution)/shard_map/all_to_all | solution.py:36
  132.5 1.2 broadcast_in_dim.62
  133.7 8.2 %all_to_all.32 = bf16[2,32,32,256]{3,2,1,0:T(8,128)(2,1)S(1)} all-to-all(bf16[2,32,32,256]{3,2,1,0:T(8,128)(2,1)S(1)} %broadcast_in_dim.62), channel_id=1, replica_groups=mesh['sector'=8,'term_0'=4,'term_1'=8,'term_2'=2] {'term_2'}, dimensions={0} | all-to-all | bytes 2097152 | tf_op jit(solution)/shard_map/all_to_all | solution.py:36
  142.2 0.9 copy-done.2
  143.2 4.2 %select_reduce_fusion = (f32[2]{0:T(128)S(1)}, f32[2,256,256]{2,1,0:T(8,128)S(1)}) fusion(pred[256,256]{1,0:T(8,128)(4,1)S(1)} %iota_compare_fusion, f32[2,1024,256]{2,1,0:T(8,128)S(1)} %bitcast.84, bf16[2,1024,256]{2,1,0:T(8,128)(2,1)S(1)} %copy-done.2, pred[2,1024]{1,0:T(4,128)(4,1)S(1)} %iota_compare_fusion.1), kind=kOutput, calls=%fused_computation.36 | convolution fusion | flops 1612447744 | bytes 3737608 | tf_op jit(solution)/shard_map/sia,sib->sab/dot_general | solution.py:120
  147.4 0.7 fusion.11
  148.1 0.7 fusion.24
  148.8 0.6 fusion.18
  149.5 0.7 fusion.10
  150.1 0.7 fusion.28
  150.8 0.7 fusion.27
  151.5 0.7 fusion.9
  152.1 0.7 fusion.30
  152.8 0.7 fusion.29
  153.4 0.7 fusion.8
  154.1 0.7 fusion.32
  154.8 0.9 fusion.31
  155.6 0.7 fusion.7
  156.3 0.7 fusion.34
  157.0 0.7 fusion.33
  157.6 0.7 fusion.6
  158.3 0.7 fusion.36
  159.0 0.7 fusion.35
  159.6 0.7 fusion.5
  160.3 0.7 fusion.38
  160.9 0.7 fusion.37
  161.6 0.7 fusion.4
  162.3 0.7 fusion.39
  162.9 2.2 multiply_convert_fusion
  165.3 54.8 %all_to_all.33 = bf16[8,2,256,256]{3,2,1,0:T(8,128)(2,1)} all-to-all(bf16[8,2,256,256]{3,2,1,0:T(8,128)(2,1)S(1)} %broadcast_in_dim.67), channel_id=1, replica_groups=mesh['sector'=8,'term_0'=4,'term_1'=8,'term_2'=2] {'sector'}, dimensions={0} | all-to-all | bytes 4194304 | tf_op jit(solution)/shard_map/all_to_all | solution.py:36
  220.2 3.1 %gather_fusion.1 = bf16[6,256,256]{2,1,0:T(8,128)(2,1)} fusion(bf16[16,256,256]{2,1,0:T(8,128)(2,1)} %bitcast.89, s32[1024]{0:T(1024)S(1)} %pad_clamp_fusion), kind=kCustom, calls=%fused_computation.1 | custom fusion | bytes 1572888 | tf_op jit(solution)/shard_map/gather | solution.py:139
  223.3 4.0 %fusion.3 = f32[2,3,256,256]{2,3,1,0:T(8,128)} fusion(bf16[2,3,256,256]{3,2,1,0:T(8,128)(2,1)} %bitcast.90, bf16[2,3,1024,256]{3,2,1,0:T(8,128)(2,1)S(1)} %copy-done, bf16[2,1024,256]{2,1,0:T(8,128)(2,1)} %copy-done.1), kind=kOutput, calls=%fused_computation.11 | convolution fusion | flops 1007026176 | bytes 6553600 | tf_op jit(solution)/shard_map/spab,spbc->spac/dot_general | solution.py:143
  227.3 1.4 select_convert_fusion
  228.7 3.9 %collective-permute-start.2 = (bf16[2,3,256,2,64]{2,4,3,1,0:T(8,128)(2,1)S(1)}, bf16[2,3,256,2,64]{2,4,3,1,0:T(8,128)(2,1)S(1)}, u32[]{:S(2)}, u32[]{:S(2)}) collective-permute-start(bf16[2,3,256,2,64]{2,4,3,1,0:T(8,128)(2,1)S(1)} %select_convert_fusion), channel_id=1, source_target_pairs={{0,2},{2,0},{1,3},{3,1},{4,6},{6,4},{5,7},{7,5},{8,10},{10,8},{9,1... | collective-permute-start | bytes 1179656 | tf_op jit(solution)/shard_map/ppermute | solution.py:25
  232.7 9.1 %collective-permute-done.2 = bf16[2,3,256,2,64]{2,4,3,1,0:T(8,128)(2,1)S(1)} collective-permute-done((bf16[2,3,256,2,64]{2,4,3,1,0:T(8,128)(2,1)S(1)}, bf16[2,3,256,2,64]{2,4,3,1,0:T(8,128)(2,1)S(1)}, u32[]{:S(2)}, u32[]{:S(2)}) %collective-permute-start.2) | collective-permute-done | bytes 393248 | tf_op jit(solution)/shard_map/ppermute | solution.py:25
  241.7 1.5 convert_add_fusion
  243.3 0.9 copy-done.3
  244.2 2.9 %collective-permute-start.3 = (bf16[2,3,256,1,64]{2,4,3,1,0:T(8,128)(2,1)S(1)}, bf16[2,3,256,1,64]{2,4,3,1,0:T(8,128)(2,1)S(1)}, u32[]{:S(2)}, u32[]{:S(2)}) collective-permute-start(bf16[2,3,256,1,64]{2,4,3,1,0:T(8,128)(2,1)S(1)} %select_convert_fusion.1), channel_id=1, source_target_pairs={{0,1},{1,0},{2,3},{3,2},{4,5},{5,4},{6,7},{7,6},{8,9},{9,8},{10,11... | collective-permute-start | bytes 589832 | tf_op jit(solution)/shard_map/ppermute | solution.py:25
  247.1 1.3 constant_dynamic-slice_fusion.1
  248.4 1.9 fusion.21
  (24 shorter events, 0.9 us)
Async XLA Ops:
  0.6 62.2 %copy-start = (bf16[2,3,1024,256]{3,2,1,0:T(8,128)(2,1)S(1)}, bf16[2,3,1024,256]{3,2,1,0:T(8,128)(2,1)}, u32[]{:S(2)}) copy-start(bf16[2,3,1024,256]{3,2,1,0:T(8,128)(2,1)} %param.6) | copy-start | bytes 9437188
  3.3 7.8 %copy-start.5 = (bf16[2,3,256,64]{2,3,1,0:T(8,128)(2,1)S(1)}, bf16[2,3,256,64]{2,3,1,0:T(8,128)(2,1)}, u32[]{:S(2)}) copy-start(bf16[2,3,256,64]{2,3,1,0:T(8,128)(2,1)} %param.7) | copy-start | bytes 589828
  3.3 56.4 %all-to-all-start = ((bf16[8,2,256,256]{3,2,1,0:T(8,128)(2,1)}), bf16[8,2,256,256]{3,2,1,0:T(8,128)(2,1)}, u32[]{:S(2)}, u32[]{:S(2)}) async-start(bf16[8,2,256,256]{3,2,1,0:T(8,128)(2,1)} %broadcast_in_dim.58), calls=%async_computation | async-start | bytes 4194304 | tf_op jit(solution)/shard_map/all_to_all | solution.py:36
  11.1 6.7 %collective-permute-start = (bf16[2,3,256,1,64]{2,4,3,1,0:T(8,128)(2,1)S(1)}, bf16[2,3,256,1,64]{2,4,3,1,0:T(8,128)(2,1)}, u32[]{:S(2)}, u32[]{:S(2)}) collective-permute-start(bf16[2,3,256,1,64]{2,4,3,1,0:T(8,128)(2,1)S(1)} %bitcast.93), channel_id=1, source_target_pairs={{0,1},{1,0},{2,3},{3,2},{4,5},{5,4},{6,7},{7,6},{8,9},{9,8},{10,11... | collective-permute-start | bytes 589832 | tf_op jit(solution)/shard_map/ppermute | solution.py:25
  19.7 12.5 %collective-permute-start.1 = (bf16[2,3,256,2,64]{2,4,3,1,0:T(8,128)(2,1)}, bf16[2,3,256,2,64]{2,4,3,1,0:T(8,128)(2,1)}, u32[]{:S(2)}, u32[]{:S(2)}) collective-permute-start(bf16[2,3,256,2,64]{2,4,3,1,0:T(8,128)(2,1)} %pad_maximum_fusion.1), channel_id=1, source_target_pairs={{0,2},{2,0},{1,3},{3,1},{4,6},{6,4},{5,7},{7,5},{8,10},{10,8},{9,1... | collective-permute-start | bytes 1179656 | tf_op jit(solution)/shard_map/ppermute | solution.py:25
  78.7 39.8 %copy-start.6 = (s32[16]{0:T(128)S(1)}, s32[16]{0:T(128)}, u32[]{:S(2)}) copy-start(s32[16]{0:T(128)} %param.9) | copy-start | bytes 196
  110.3 22.3 %all-to-all-start.3 = ((bf16[32,32,256]{2,1,0:T(8,128)(2,1)}), bf16[32,32,256]{2,1,0:T(8,128)(2,1)}, u32[]{:S(2)}, u32[]{:S(2)}) async-start(bf16[32,32,256]{2,1,0:T(8,128)(2,1)} %broadcast_in_dim.61), calls=%async_computation.3 | async-start | bytes 1048576 | tf_op jit(solution)/shard_map/all_to_all | solution.py:36
  141.9 1.2 copy-start.2
  142.2 5.2 %copy-start.4 = (f32[256,256]{1,0:T(8,128)S(1)}, f32[256,256]{1,0:T(8,128)}, u32[]{:S(2)}) copy-start(f32[256,256]{1,0:T(8,128)} %fusion.22) | copy-start | bytes 786436
  165.1 55.1 %copy-start.1 = (bf16[2,1024,256]{2,1,0:T(8,128)(2,1)}, bf16[2,1024,256]{2,1,0:T(8,128)(2,1)S(1)}, u32[]{:S(2)}) copy-start(bf16[2,1024,256]{2,1,0:T(8,128)(2,1)S(1)} %multiply_convert_fusion) | copy-start | bytes 3145732
  228.7 13.0 %collective-permute-start.2 = (bf16[2,3,256,2,64]{2,4,3,1,0:T(8,128)(2,1)S(1)}, bf16[2,3,256,2,64]{2,4,3,1,0:T(8,128)(2,1)S(1)}, u32[]{:S(2)}, u32[]{:S(2)}) collective-permute-start(bf16[2,3,256,2,64]{2,4,3,1,0:T(8,128)(2,1)S(1)} %select_convert_fusion), channel_id=1, source_target_pairs={{0,2},{2,0},{1,3},{3,1},{4,6},{6,4},{5,7},{7,5},{8,10},{10,8},{9,1... | collective-permute-start | bytes 1179656 | tf_op jit(solution)/shard_map/ppermute | solution.py:25
  243.2 0.9 copy-start.3
  244.2 4.3 %collective-permute-start.3 = (bf16[2,3,256,1,64]{2,4,3,1,0:T(8,128)(2,1)S(1)}, bf16[2,3,256,1,64]{2,4,3,1,0:T(8,128)(2,1)S(1)}, u32[]{:S(2)}, u32[]{:S(2)}) collective-permute-start(bf16[2,3,256,1,64]{2,4,3,1,0:T(8,128)(2,1)S(1)} %select_convert_fusion.1), channel_id=1, source_target_pairs={{0,1},{1,0},{2,3},{3,2},{4,5},{5,4},{6,7},{7,6},{8,9},{9,8},{10,11... | collective-permute-start | bytes 589832 | tf_op jit(solution)/shard_map/ppermute | solution.py:25
where the time goes:
time: 251 us; the launch traced here: 250 us
  blocking collectives  98.8 us (39%)
  waiting for transfers between devices  58.5 us (23%)
  starting transfers between devices  30.3 us (12%)
  matrix products  29.4 us (12%)
  local copies, waits for them, and re-layouts  18 us (7%)
  other arithmetic  14.2 us (6%)
    all_to_all x2, blocking collectives, copy_for_each(): return lax.all_to_all(copies, axis, split_axis=0, concat_axis=0, tiled=True)  63.1 us
    all_to_all x2, waiting for transfers between devices, copy_for_each(): return lax.all_to_all(copies, axis, split_axis=0, concat_axis=0, tiled=True)  38.6 us
    all_to_all x1, blocking collectives, sum_by_axis(): lax.all_to_all(own.astype(jnp.bfloat16), far, 0, 0, tiled=True)  27.1 us
    ppermute x4, waiting for transfers between devices, from_partner(): return lax.ppermute(block, axis, route)  19.9 us
    all_to_all x2, starting transfers between devices, copy_for_each(): return lax.all_to_all(copies, axis, split_axis=0, concat_axis=0, tiled=True)  16 us
    ppermute x4, starting transfers between devices, from_partner(): return lax.ppermute(block, axis, route)  14.3 us
    all_to_all x1, blocking collectives, summed_on_arrival(): pieces = lax.all_to_all(split_up(shard, dim, peers), axis, 0, 0, tiled=True)  8.63 us
    dot_general x8, matrix products, body(): jnp.einsum('sab,sbc->sac', ns_factor, inverse_part, precision=highest)  5.42 us
  transfers between devices with their start and end apart: 6, of which 5 were waited for; matrix products, arithmetic and copies ran while one was open for 3% of the time, Pallas kernels for 0%

commit v1 on v0

v1 whole, which is shorter than its diff:
```python
import jax
import jax.numpy as jnp
from jax import lax
from jax.experimental import pallas as pl
from jax.experimental.pallas import tpu as pltpu
from jax.sharding import Mesh
from jax.sharding import PartitionSpec as P

STEPS = 8
NY, NX, NZ = 8, 4, 8
ROWS, COLS, HALF = 1024, 256, 128
TERM = ("x", "z", "core")
STEP_SIZE = 0.15
EPSILON = 1e-06
MESH = pl.DeviceIdType.MESH
F32, BF16 = jnp.float32, jnp.bfloat16
FAR_FIRST = (4, 3, 5, 2, 6, 1, 7, 0)


def dot(a, b):
    return jnp.dot(a, b, preferred_element_type=F32)


def dot_over_rows(a, b):
    return lax.dot_general(a, b, (((0,), (0,)), ((), ())), preferred_element_type=F32)


def two_parts(a):
    high = a.astype(BF16)
    return high, (a - high.astype(F32)).astype(BF16)


def dot3(a, b):
    return dot(a[0], b[0]) + (dot(a[0], b[1]) + dot(a[1], b[0]))


def remote(src, dst, send, recv, to):
    return pltpu.make_async_remote_copy(
        src_ref=src, dst_ref=dst, send_sem=send, recv_sem=recv, device_id=to, device_id_type=MESH
    )


class Gather:
    def __init__(self, pos, blocks, sems):
        self.pos, self.blocks = pos, blocks
        self.y_send, self.y_recv, self.x_send, self.x_recv = sems
        self.half = lax.rem(pos["x"], 2)
        self.started = []

    def place(self, way, d, j, half):
        y, core = self.pos["sector"], self.pos["core"]
        step = d if way == 0 else NY - d
        sector = core if j == 0 else 1 - core
        index = 2 * lax.rem(y - step + 2 * NY, NY) + sector
        return self.blocks.at[index, pl.ds(pl.multiple_of(half * HALF, HALF), HALF), :]

    def to_y(self, way):
        y = self.pos["sector"]
        return {**self.pos, "sector": lax.rem(y + (1 if way == 0 else NY - 1), NY)}

    def to_x(self, j):
        x = self.pos["x"]
        return {**self.pos, "x": lax.rem(x + (1 if j == 0 else NX - 1), NX)}

    def go(self, copy):
        copy.start()
        self.started.append(copy)

    def start(self, j, source):
        for way in (0, 1):
            self.go(
                remote(
                    source,
                    self.place(way, 0, j, self.half),
                    self.y_send.at[way, 0, j],
                    self.y_recv.at[way, 0, j],
                    self.to_y(way),
                )
            )

    def arrive(self, d):
        for j in (0, 1):
            for way in (0, 1):
                if d == 4 and j != way:
                    continue
                block = self.place(way, d, j, self.half)
                remote(
                    block,
                    block,
                    self.y_send.at[way, d - 1, j],
                    self.y_recv.at[way, d - 1, j],
                    self.to_y(way),
                ).wait_recv()
                if d < 3 or (d == 3 and j == way):
                    self.go(
                        remote(
                            block,
                            block,
                            self.y_send.at[way, d, j],
                            self.y_recv.at[way, d, j],
                            self.to_y(way),
                        )
                    )
                self.go(
                    remote(
                        block,
                        block,
                        self.x_send.at[way, d - 1, j],
                        self.x_recv.at[way, d - 1, j],
                        self.to_x(j),
                    )
                )

    def finish(self):
        for d in (1, 2, 3, 4):
            for j in (0, 1):
                for way in (0, 1):
                    if d == 4 and j != way:
                        continue
                    block = self.place(way, d, j, 1 - self.half)
                    remote(
                        block,
                        block,
                        self.x_send.at[way, d - 1, j],
                        self.x_recv.at[way, d - 1, j],
                        self.to_x(j),
                    ).wait_recv()


def kernel(
    shift,
    live,
    wave,
    left,
    right,
    iso_out,
    env_out,
    left_v,
    wave_v,
    wave_all,
    right_all,
    right_full,
    applied,
    sib_out,
    sib_in,
    sigma,
    x_out,
    x_own,
    x_in,
    z_out,
    z_own,
    z_in,
    total,
    u_high,
    u_low,
    root,
    inverse,
    iso,
    iso_all,
    front,
    e_out,
    e_in,
    e_own,
    ez_out,
    ez_in,
    local_sem,
    r_send,
    r_recv,
    sib_send,
    sib_recv,
    xs_send,
    xs_recv,
    zs_send,
    zs_recv,
    gz_send,
    gz_recv,
    gx_send,
    gx_recv,
    i_send,
    i_recv,
    e_send,
    e_recv,
    ez_send,
    ez_recv,
    *ring_sems,
):
    y, x, z, core = (lax.axis_index(a) for a in ("sector", "x", "z", "core"))
    pos = {"sector": y, "x": x, "z": z, "core": core}
    zb = lax.rem(z, 2)
    part = 2 * zb + core
    group = 4 * x + z // 2
    half = lax.rem(x, 2)
    other = 1 - core
    sibling = {**pos, "core": other}
    z_pair = {**pos, "z": z + 1 - 2 * zb}
    x_to = [{**pos, "x": lax.rem(x + dx, NX)} for dx in range(NX)]
    z_to = [{**pos, "z": lax.rem(z + dz, NZ)} for dz in range(NZ)]
    sectors = (core, other)
    waits = []

    def go(copy):
        copy.start()
        waits.append(copy)
        return copy

    part_row = pl.multiple_of(part * COLS, COLS)
    own_left = pltpu.make_async_copy(left, left_v, local_sem.at[0])
    own_wave = pltpu.make_async_copy(wave.at[core], wave_v, local_sem.at[1])
    own_block = pltpu.make_async_copy(
        wave.at[:, pl.ds(part_row, COLS), :], wave_all.at[pl.ds(2 * y, 2)], local_sem.at[2]
    )
    own_block.start()
    own_left.start()
    own_wave.start()

    barrier = pltpu.get_barrier_semaphore()
    partners = (
        [{**pos, "sector": lax.rem(y + k, NY)} for k in (1, NY - 1)] + x_to[1:] + z_to[1:] + [sibling]
    )
    for to in partners:
        pl.semaphore_signal(barrier, inc=1, device_id=to, device_id_type=MESH)
    for term in range(3):
        right_all[part, term] = jnp.concatenate([right[0, term], right[1, term]], axis=1)
    pl.semaphore_wait(barrier, len(partners))

    first = Gather(pos, wave_all, ring_sems[:4])
    send_row = pl.multiple_of(part * COLS + half * HALF, HALF)
    for j in (0, 1):
        first.start(j, wave.at[sectors[j], pl.ds(send_row, HALF), :])
    mine = right_all.at[part]
    go(remote(mine, mine, r_send.at[0], r_recv.at[0], sibling))
    go(remote(mine, mine, r_send.at[1], r_recv.at[1], z_pair))
    first.arrive(1)
    far = right_all.at[2 * (1 - zb) + core]
    remote(far, far, r_send.at[1], r_recv.at[1], z_pair).wait_recv()
    go(remote(far, far, r_send.at[2], r_recv.at[2], sibling))
    first.arrive(2)
    near = right_all.at[2 * zb + other]
    remote(near, near, r_send.at[0], r_recv.at[0], sibling).wait_recv()
    last = right_all.at[2 * (1 - zb) + other]
    remote(last, last, r_send.at[2], r_recv.at[2], sibling).wait_recv()
    low_lanes = lax.broadcasted_iota(jnp.int32, (COLS, 128), 1) < 64
    for term in range(3):
        for a in (0, 1):
            one = right_all[2 * a, term].astype(F32)
            two = right_all[2 * a + 1, term].astype(F32)
            lanes = slice(128 * a, 128 * (a + 1))
            right_full[0, term, :, lanes] = jnp.where(low_lanes, one, pltpu.roll(two, 64, 1)).astype(BF16)
            right_full[1, term, :, lanes] = jnp.where(low_lanes, pltpu.roll(one, 64, 1), two).astype(BF16)
    first.arrive(3)
    first.arrive(4)
    own_left.wait()
    own_wave.wait()
    own_block.wait()
    first.finish()

    for s in (other, core):
        for term in range(3):
            source = shift[3 * group + term, 2 * y + s]
            applied[s, term] = dot(wave_all[source], right_full[s, term]).astype(BF16)
        for q in range(4):
            rows = slice(256 * q, 256 * (q + 1))
            acc = dot(left_v[s, 0, rows, :], applied[s, 0])
            for term in (1, 2):
                acc = acc + dot(left_v[s, term, rows, :], applied[s, term])
            if s is other:
                sib_out[rows, :] = acc.astype(BF16)
                if q % 2 == 1:
                    h = pl.ds(512 * (q // 2), 512)
                    go(remote(sib_out.at[h], sib_in.at[h], sib_send.at[q // 2], sib_recv.at[q // 2], sibling))
            else:
                sigma[rows, :] = acc
    for q in (0, 1):
        h = pl.ds(512 * q, 512)
        remote(sib_out.at[h], sib_in.at[h], sib_send.at[q], sib_recv.at[q], sibling).wait_recv()

    def partial(dx, dz):
        at = 256 * lax.rem(x + dx, NX) + 32 * lax.rem(z + dz, NZ)
        rows = pl.ds(pl.multiple_of(at, 32), 32)
        return sigma[rows, :] + sib_in[rows, :].astype(F32)

    for g in range(4):
        for dx in (2, 1, 3):
            for i in (2 * g, 2 * g + 1):
                x_out[dx - 1, 32 * i : 32 * (i + 1), :] = partial(dx, FAR_FIRST[i]).astype(BF16)
            h = pl.ds(64 * g, 64)
            go(
                remote(
                    x_out.at[dx - 1, h],
                    x_in.at[dx - 1, h],
                    xs_send.at[dx - 1, g],
                    xs_recv.at[dx - 1, g],
                    x_to[dx],
                )
            )
    for i in range(8):
        x_own[32 * i : 32 * (i + 1), :] = partial(0, FAR_FIRST[i])
    for g in range(4):
        rows = slice(64 * g, 64 * (g + 1))
        acc = x_own[rows, :]
        for dx in (1, 2, 3):
            h = pl.ds(64 * g, 64)
            remote(
                x_out.at[dx - 1, h], x_in.at[dx - 1, h], xs_send.at[dx - 1, g], xs_recv.at[dx - 1, g], x_to[dx]
            ).wait_recv()
            acc = acc + x_in[dx - 1, rows, :].astype(F32)
        for i in (2 * g, 2 * g + 1):
            piece = acc[32 * (i % 2) : 32 * (i % 2 + 1), :]
            if FAR_FIRST[i]:
                z_out[i] = piece.astype(BF16)
                go(remote(z_out.at[i], z_in.at[i], zs_send.at[i], zs_recv.at[i], z_to[FAR_FIRST[i]]))
            else:
                z_own[...] = piece
    acc = z_own[...]
    for i in range(7):
        remote(z_out.at[i], z_in.at[i], zs_send.at[i], zs_recv.at[i], z_to[FAR_FIRST[i]]).wait_recv()
        acc = acc + z_in[i].astype(F32)

    def piece_at(dx, dz):
        at = 256 * lax.rem(x + NX - dx, NX) + 32 * lax.rem(z + NZ - dz, NZ)
        return total.at[pl.ds(pl.multiple_of(at, 32), 32)]

    own_piece = piece_at(0, 0)
    own_piece[...] = acc.astype(BF16)
    for i in range(7):
        go(remote(own_piece, own_piece, gz_send.at[i], gz_recv.at[i], z_to[FAR_FIRST[i]]))
    for i in range(7, -1, -1):
        piece = piece_at(0, FAR_FIRST[i])
        if i < 7:
            remote(piece, piece, gz_send.at[i], gz_recv.at[i], z_to[FAR_FIRST[i]]).wait_recv()
        for dx in (2, 1, 3):
            go(remote(piece, piece, gx_send.at[dx - 1, i], gx_recv.at[dx - 1, i], x_to[dx]))
    for i in range(7, -1, -1):
        for dx in (1, 2, 3):
            piece = piece_at(dx, FAR_FIRST[i])
            remote(piece, piece, gx_send.at[dx - 1, i], gx_recv.at[dx - 1, i], x_to[dx]).wait_recv()

    limit = live[2 * y + core]
    gram = jnp.zeros((COLS, COLS), F32)
    cross = jnp.zeros((COLS, COLS), F32)
    for q in range(4):
        rows = slice(256 * q, 256 * (q + 1))
        row_ids = 256 * q + lax.broadcasted_iota(jnp.int32, (256, COLS), 0)
        value = wave_v[rows, :].astype(F32) - STEP_SIZE * total[rows, :].astype(F32)
        high, low = two_parts(jnp.where(row_ids < limit, value, 0.0))
        u_high[rows, :] = high
        u_low[rows, :] = low
        gram = gram + dot_over_rows(high, high)
        cross = cross + dot_over_rows(high, low)
    gram = gram + (cross + cross.T)
    diagonal = lax.broadcasted_iota(jnp.int32, (COLS, COLS), 0) == lax.broadcasted_iota(jnp.int32, (COLS, COLS), 1)
    trace = jnp.sum(jnp.where(diagonal, gram, 0.0), keepdims=True) + EPSILON
    three_halves = jnp.where(diagonal, 1.5, 0.0)
    y0 = gram / trace
    factor = three_halves - 0.5 * y0
    root[...] = dot3(two_parts(y0), two_parts(factor))
    inverse[...] = factor

    def newton_schulz(_, carry):
        y_parts, z_parts = two_parts(root[...]), two_parts(inverse[...])
        f_parts = two_parts(three_halves - 0.5 * dot3(z_parts, y_parts))
        root[...] = dot3(y_parts, f_parts)
        inverse[...] = dot3(f_parts, z_parts)
        return carry

    lax.fori_loop(0, STEPS - 2, newton_schulz, 0)
    y_parts, z_parts = two_parts(root[...]), two_parts(inverse[...])
    f_parts = two_parts(three_halves - 0.5 * dot3(z_parts, y_parts))
    z_parts = two_parts(dot3(f_parts, z_parts))
    scale = jnp.sqrt(ROWS / trace)

    second = Gather(pos, iso_all, ring_sems[4:])
    for h in (0, 1):
        base = pl.multiple_of(512 * (zb if h == 0 else 1 - zb), 512)
        for q in (0, 1):
            rows = pl.ds(base + 256 * q, 256)
            a = (u_high[rows, :], u_low[rows, :])
            iso[core, rows, :] = (dot3(a, z_parts) * scale).astype(BF16)
        block = iso.at[core, pl.ds(base, 512)]
        go(remote(block, block, i_send.at[h], i_recv.at[h], sibling))
        if h == 0:
            second.start(0, iso.at[core, pl.ds(send_row, HALF), :])

    def from_sibling(h):
        base = pl.multiple_of(512 * (zb if h == 0 else 1 - zb), 512)
        block = iso.at[other, pl.ds(base, 512)]
        remote(block, block, i_send.at[h], i_recv.at[h], sibling).wait_recv()

    from_sibling(0)
    second.start(1, iso.at[other, pl.ds(send_row, HALF), :])

    def project(s):
        for term in range(3):
            front[s, term] = dot_over_rows(iso[s], left_v[s, term]).astype(BF16)

    project(core)
    second.arrive(1)
    from_sibling(1)
    project(other)
    second.arrive(2)
    for s in (0, 1):
        iso_all[2 * y + s] = iso[s, pl.ds(part_row, COLS), :]
        iso_out[s] = iso[s, pl.ds(pl.multiple_of(16 * (2 * (NZ * x + z) + core), 16), 16), :]
    second.arrive(3)
    second.arrive(4)
    second.finish()

    for term in range(3):
        values = [
            dot(front[s, term], iso_all[shift[3 * group + term, 2 * y + s]]) * (1 / 32) for s in (0, 1)
        ]
        for a in (0, 1):
            one, two = (v[:, 128 * a : 128 * (a + 1)] for v in values)
            for_zero = jnp.where(low_lanes, one, pltpu.roll(two, 64, 1))
            for_one = jnp.where(low_lanes, pltpu.roll(one, 64, 1), two)
            e_own[a, term] = jnp.where(core == 0, for_zero, for_one)
            e_out[term, a] = jnp.where(core == 0, for_one, for_zero).astype(BF16)
        go(remote(e_out.at[term], e_in.at[term], e_send.at[term], e_recv.at[term], sibling))
    for term in range(3):
        remote(e_out.at[term], e_in.at[term], e_send.at[term], e_recv.at[term], sibling).wait_recv()
        ez_out[term] = (e_own[1 - zb, term] + e_in[term, 1 - zb].astype(F32)).astype(BF16)
        go(remote(ez_out.at[term], ez_in.at[term], ez_send.at[term], ez_recv.at[term], z_pair))
    for term in range(3):
        kept = e_own[zb, term] + e_in[term, zb].astype(F32)
        remote(ez_out.at[term], ez_in.at[term], ez_send.at[term], ez_recv.at[term], z_pair).wait_recv()
        kept = kept + ez_in[term].astype(F32)
        env_out[0, term] = kept[:, :64].astype(BF16)
        env_out[1, term] = pltpu.roll(kept, 64, 1)[:, :64].astype(BF16)

    for copy in waits + first.started + second.started:
        copy.wait_send()


def body(wave_in, left_env, right_env, shift_map, live_rows):
    dma = pltpu.SemaphoreType.DMA
    vmem, smem, anywhere = (pl.BlockSpec(memory_space=m) for m in (pltpu.VMEM, pltpu.SMEM, pl.ANY))
    scratch = [
        pltpu.VMEM((2, 3, ROWS, COLS), BF16),
        pltpu.VMEM((ROWS, COLS), BF16),
        pltpu.VMEM((16, COLS, COLS), BF16),
        pltpu.VMEM((4, 3, COLS, 128), BF16),
        pltpu.VMEM((2, 3, COLS, COLS), BF16),
        pltpu.VMEM((2, 3, COLS, COLS), BF16),
        pltpu.VMEM((ROWS, COLS), BF16),
        pltpu.VMEM((ROWS, COLS), BF16),
        pltpu.VMEM((ROWS, COLS), F32),
        pltpu.VMEM((3, 256, COLS), BF16),
        pltpu.VMEM((256, COLS), F32),
        pltpu.VMEM((3, 256, COLS), BF16),
        pltpu.VMEM((7, 32, COLS), BF16),
        pltpu.VMEM((32, COLS), F32),
        pltpu.VMEM((7, 32, COLS), BF16),
        pltpu.VMEM((ROWS, COLS), BF16),
        pltpu.VMEM((ROWS, COLS), BF16),
        pltpu.VMEM((ROWS, COLS), BF16),
        pltpu.VMEM((COLS, COLS), F32),
        pltpu.VMEM((COLS, COLS), F32),
        pltpu.VMEM((2, ROWS, COLS), BF16),
        pltpu.VMEM((16, COLS, COLS), BF16),
        pltpu.VMEM((2, 3, COLS, COLS), BF16),
        pltpu.VMEM((3, 2, COLS, 128), BF16),
        pltpu.VMEM((3, 2, COLS, 128), BF16),
        pltpu.VMEM((2, 3, COLS, 128), F32),
        pltpu.VMEM((3, COLS, 128), BF16),
        pltpu.VMEM((3, COLS, 128), BF16),
        dma((3,)),
        *[dma((3,))] * 2,
        *[dma((2,))] * 2,
        *[dma((3, 4))] * 2,
        *[dma((7,))] * 2,
        *[dma((7,))] * 2,
        *[dma((3, 8))] * 2,
        *[dma((2,))] * 2,
        *[dma((3,))] * 2,
        *[dma((3,))] * 2,
        *[dma((2, 4, 2))] * 8,
    ]
    return pl.pallas_call(
        kernel,
        out_shape=(
            jax.ShapeDtypeStruct((2, 16, COLS), BF16),
            jax.ShapeDtypeStruct((2, 3, COLS, 64), BF16),
        ),
        in_specs=[smem, smem, anywhere, anywhere, vmem],
        out_specs=(vmem, vmem),
        scratch_shapes=scratch,
        compiler_params=pltpu.CompilerParams(
            collective_id=0, has_side_effects=True, vmem_limit_bytes=40 * 2**20
        ),
        cost_estimate=pl.CostEstimate(flops=8 * 10**9, bytes_accessed=8 * 2**20, transcendentals=0),
        name="dmrg_window",
    )(shift_map, live_rows, wave_in, left_env, right_env)


def solution(mesh):
    split = Mesh(mesh.devices.reshape(NY, NX, NZ, 2), ("sector", *TERM))
    return jax.shard_map(
        body,
        mesh=split,
        in_specs=(
            P("sector", None, None),
            P("sector", TERM, None, None),
            P("sector", TERM, None, None),
            P(),
            P(),
        ),
        out_specs=(P("sector", TERM, None), P("sector", TERM, None, None)),
        check_vma=False,
    )
```

time: 251 us -> 102 us (0.41)
  blocking collectives: 98.8 us -> 0 us
  Pallas kernels: 0 us -> 94 us
  waiting for transfers between devices: 58.5 us -> 0 us
  starting transfers between devices: 30.3 us -> 0 us
  matrix products: 29.4 us -> 0 us
  other arithmetic: 14.2 us -> 0 us
  local copies, waits for them, and re-layouts: 18 us -> 7.14 us
    all_to_all x4 -> x0, blocking collectives: 98.8 us -> none  [the longest x2 63.1 us: copy_for_each(): return lax.all_to_all(copies, axis, split_axis=0, concat_axis=0, tiled=True)]
    pallas_call x0 -> x1, Pallas kernels: none -> 94 us  [body(): pl.pallas_call(kernel, out_shape=(jax.ShapeDtypeStruct((2, 16, COLS), BF1...]
    all_to_all x2 -> x0, waiting for transfers between devices: 38.6 us -> none  [copy_for_each(): return lax.all_to_all(copies, axis, split_axis=0, concat_axis=0, tiled=True)]
    dot_general x27 -> x0, matrix products: 29.4 us -> none  [the longest x8 5.42 us: body(): jnp.einsum('sab,sbc->sac', ns_factor, inverse_part, precision=highest)]
    ppermute x4 -> x0, waiting for transfers between devices: 19.9 us -> none  [from_partner(): return lax.ppermute(block, axis, route)]
    all_to_all x2 -> x0, starting transfers between devices: 16 us -> none  [copy_for_each(): return lax.all_to_all(copies, axis, split_axis=0, concat_axis=0, tiled=True)]
    ppermute x4 -> x0, starting transfers between devices: 14.3 us -> none  [from_partner(): return lax.ppermute(block, axis, route)]
    gather x2 -> x0, local copies, waits for them, and re-layouts: 6.2 us -> none  [the longest x1 3.1 us: body(): picked_wave = every_source[sources]]
  transfers between devices with their start and end apart: 6 -> 0, of which waited for: 5 -> 0; matrix products, arithmetic and copies ran while one was open for 3% -> 0% of each run, Pallas kernels for 0% -> 0%
where the time goes in v1:
time: 102 us
  Pallas kernels  94 us (92%)
  local copies, waits for them, and re-layouts  7.14 us (7%)
    pallas_call x1, Pallas kernels, body(): pl.pallas_call(kernel, out_shape=(jax.ShapeDtypeStruct((2, 16, COLS), BF1...  94 us
    unnamed x9, local copies, waits for them, and re-layouts  6.29 us

profile of v1, /device:TPU:1, one launch (start us, length us, event | category | flops | bytes accessed | tf_op | source)
XLA Modules:
  0.0 101.8 jit_solution(18281793768097277574)
XLA Ops:
  0.6 0.8 copy.7.shift
  1.4 1.1 %copy.8.right = bf16[2,3,256,64]{3,2,1,0:T(8,128)(2,1)S(1)} copy(bf16[2,3,256,64]{2,3,1,0:T(8,128)(2,1)} %param.7) | data formatting | bytes 393216 | tf_op args[2]
  2.6 0.0 copy-start
  2.6 1.9 %copy-done = bf16[2,3,1024,256]{3,2,1,0:T(8,128)(2,1)S(1)} copy-done((bf16[2,3,1024,256]{3,2,1,0:T(8,128)(2,1)S(1)}, bf16[2,3,1024,256]{3,2,1,0:T(8,128)(2,1)}, u32[]{:S(2)}) %copy-start) | copy-done | bytes 3145752
  4.5 0.0 copy-start.1
  4.5 1.2 %copy-done.1 = bf16[2,1024,256]{2,1,0:T(8,128)(2,1)S(1)} copy-done((bf16[2,1024,256]{2,1,0:T(8,128)(2,1)S(1)}, bf16[2,1024,256]{2,1,0:T(8,128)(2,1)}, u32[]{:S(2)}) %copy-start.1) | copy-done | bytes 1048600
  5.7 0.0 copy-start.2
  5.7 0.7 copy-done.2
  6.3 94.0 %dmrg_window.1 = (bf16[2,16,256]{2,1,0:T(8,128)(2,1)S(1)}, bf16[2,3,256,64]{3,2,1,0:T(8,128)(2,1)S(1)}) custom-call(s32[48,16]{1,0:T(8,128)S(1)} %copy.7.shift, s32[16]{0:T(128)S(1)} %copy-done.2, bf16[2,1024,256]{2,1,0:T(8,128)(2,1)S(1)} %copy-done.1, bf16[2,3,1024,256]{3,2,1,0:T(8,128)(2,1)S(1)} %copy-done, bf16[2,3,256,64]{3,2,1,0:T(8,128)(2,1)S(1)} %copy.8.right), custom_call_target="tpu_custom_call" | custom-call | flops 8000000000 | bytes 8388608 | tf_op jit(solution)/shard_map/dmrg_window/pallas_call | solution.py:478
  100.3 0.8 copy.9
  101.2 0.6 copy.11
Async XLA Ops:
  2.6 1.9 %copy-start = (bf16[2,3,1024,256]{3,2,1,0:T(8,128)(2,1)S(1)}, bf16[2,3,1024,256]{3,2,1,0:T(8,128)(2,1)}, u32[]{:S(2)}) copy-start(bf16[2,3,1024,256]{3,2,1,0:T(8,128)(2,1)} %left.1) | copy-start | bytes 9437188
  4.5 1.2 %copy-start.1 = (bf16[2,1024,256]{2,1,0:T(8,128)(2,1)S(1)}, bf16[2,1024,256]{2,1,0:T(8,128)(2,1)}, u32[]{:S(2)}) copy-start(bf16[2,1024,256]{2,1,0:T(8,128)(2,1)} %wave.1) | copy-start | bytes 3145732
  5.7 0.7 copy-start.2

commit v2 on v1

--- a/solution.py
+++ b/solution.py
@@ -23,6 +23,10 @@
 
 def dot_over_rows(a, b):
     return lax.dot_general(a, b, (((0,), (0,)), ((), ())), preferred_element_type=F32)
+
+
+def dot_over_columns(a, b):
+    return lax.dot_general(a, b, (((1,), (1,)), ((), ())), preferred_element_type=F32)
 
 
 def two_parts(a):
@@ -139,7 +143,6 @@
     wave_v,
     wave_all,
     right_all,
-    right_full,
     applied,
     sib_out,
     sib_in,
@@ -219,45 +222,41 @@
     )
     for to in partners:
         pl.semaphore_signal(barrier, inc=1, device_id=to, device_id_type=MESH)
-    for term in range(3):
-        right_all[part, term] = jnp.concatenate([right[0, term], right[1, term]], axis=1)
     pl.semaphore_wait(barrier, len(partners))
 
     first = Gather(pos, wave_all, ring_sems[:4])
     send_row = pl.multiple_of(part * COLS + half * HALF, HALF)
     for j in (0, 1):
         first.start(j, wave.at[sectors[j], pl.ds(send_row, HALF), :])
-    mine = right_all.at[part]
-    go(remote(mine, mine, r_send.at[0], r_recv.at[0], sibling))
-    go(remote(mine, mine, r_send.at[1], r_recv.at[1], z_pair))
+    def right_rows(p):
+        return right_all.at[:, :, pl.ds(pl.multiple_of(64 * p, 64), 64), :]
+
+    mine = right_rows(part)
+    own_right = pltpu.make_async_copy(right, mine, local_sem.at[3])
+    own_right.start()
+    go(remote(right, mine, r_send.at[0], r_recv.at[0], sibling))
+    go(remote(right, mine, r_send.at[1], r_recv.at[1], z_pair))
     first.arrive(1)
-    far = right_all.at[2 * (1 - zb) + core]
+    far = right_rows(2 * (1 - zb) + core)
     remote(far, far, r_send.at[1], r_recv.at[1], z_pair).wait_recv()
     go(remote(far, far, r_send.at[2], r_recv.at[2], sibling))
     first.arrive(2)
-    near = right_all.at[2 * zb + other]
+    near = right_rows(2 * zb + other)
     remote(near, near, r_send.at[0], r_recv.at[0], sibling).wait_recv()
-    last = right_all.at[2 * (1 - zb) + other]
+    last = right_rows(2 * (1 - zb) + other)
     remote(last, last, r_send.at[2], r_recv.at[2], sibling).wait_recv()
-    low_lanes = lax.broadcasted_iota(jnp.int32, (COLS, 128), 1) < 64
-    for term in range(3):
-        for a in (0, 1):
-            one = right_all[2 * a, term].astype(F32)
-            two = right_all[2 * a + 1, term].astype(F32)
-            lanes = slice(128 * a, 128 * (a + 1))
-            right_full[0, term, :, lanes] = jnp.where(low_lanes, one, pltpu.roll(two, 64, 1)).astype(BF16)
-            right_full[1, term, :, lanes] = jnp.where(low_lanes, pltpu.roll(one, 64, 1), two).astype(BF16)
     first.arrive(3)
     first.arrive(4)
     own_left.wait()
     own_wave.wait()
     own_block.wait()
+    own_right.wait()
     first.finish()
 
     for s in (other, core):
         for term in range(3):
-            source = shift[3 * group + term, 2 * y + s]
-            applied[s, term] = dot(wave_all[source], right_full[s, term]).astype(BF16)
+            source = shift[2 * y + s, 3 * group + term]
+            applied[s, term] = dot_over_columns(wave_all[source], right_all[s, term]).astype(BF16)
         for q in range(4):
             rows = slice(256 * q, 256 * (q + 1))
             acc = dot(left_v[s, 0, rows, :], applied[s, 0])
@@ -391,7 +390,7 @@
 
     def project(s):
         for term in range(3):
-            front[s, term] = dot_over_rows(iso[s], left_v[s, term]).astype(BF16)
+            front[s, term] = dot_over_rows(left_v[s, term], iso[s]).astype(BF16)
 
     project(core)
     second.arrive(1)
@@ -406,15 +405,13 @@
     second.finish()
 
     for term in range(3):
-        values = [
-            dot(front[s, term], iso_all[shift[3 * group + term, 2 * y + s]]) * (1 / 32) for s in (0, 1)
-        ]
-        for a in (0, 1):
-            one, two = (v[:, 128 * a : 128 * (a + 1)] for v in values)
-            for_zero = jnp.where(low_lanes, one, pltpu.roll(two, 64, 1))
-            for_one = jnp.where(low_lanes, pltpu.roll(one, 64, 1), two)
-            e_own[a, term] = jnp.where(core == 0, for_zero, for_one)
-            e_out[term, a] = jnp.where(core == 0, for_one, for_zero).astype(BF16)
+        for s in (0, 1):
+            source = shift[2 * y + s, 3 * group + term]
+            value = dot_over_rows(iso_all[source], front[s, term]) * (1 / 32)
+            for a in (0, 1):
+                one, two = value[128 * a : 128 * a + 64, :], value[128 * a + 64 : 128 * (a + 1), :]
+                e_own[a, term, s] = jnp.where(core == 0, one, two)
+                e_out[term, a, s] = jnp.where(core == 0, two, one).astype(BF16)
         go(remote(e_out.at[term], e_in.at[term], e_send.at[term], e_recv.at[term], sibling))
     for term in range(3):
         remote(e_out.at[term], e_in.at[term], e_send.at[term], e_recv.at[term], sibling).wait_recv()
@@ -424,8 +421,8 @@
         kept = e_own[zb, term] + e_in[term, zb].astype(F32)
         remote(ez_out.at[term], ez_in.at[term], ez_send.at[term], ez_recv.at[term], z_pair).wait_recv()
         kept = kept + ez_in[term].astype(F32)
-        env_out[0, term] = kept[:, :64].astype(BF16)
-        env_out[1, term] = pltpu.roll(kept, 64, 1)[:, :64].astype(BF16)
+        for s in (0, 1):
+            env_out[s, term] = kept[s].astype(BF16)
 
     for copy in waits + first.started + second.started:
         copy.wait_send()
@@ -438,7 +435,6 @@
         pltpu.VMEM((2, 3, ROWS, COLS), BF16),
         pltpu.VMEM((ROWS, COLS), BF16),
         pltpu.VMEM((16, COLS, COLS), BF16),
-        pltpu.VMEM((4, 3, COLS, 128), BF16),
         pltpu.VMEM((2, 3, COLS, COLS), BF16),
         pltpu.VMEM((2, 3, COLS, COLS), BF16),
         pltpu.VMEM((ROWS, COLS), BF16),
@@ -458,12 +454,12 @@
         pltpu.VMEM((2, ROWS, COLS), BF16),
         pltpu.VMEM((16, COLS, COLS), BF16),
         pltpu.VMEM((2, 3, COLS, COLS), BF16),
-        pltpu.VMEM((3, 2, COLS, 128), BF16),
-        pltpu.VMEM((3, 2, COLS, 128), BF16),
-        pltpu.VMEM((2, 3, COLS, 128), F32),
-        pltpu.VMEM((3, COLS, 128), BF16),
-        pltpu.VMEM((3, COLS, 128), BF16),
-        dma((3,)),
+        pltpu.VMEM((3, 2, 2, 64, COLS), BF16),
+        pltpu.VMEM((3, 2, 2, 64, COLS), BF16),
+        pltpu.VMEM((2, 3, 2, 64, COLS), F32),
+        pltpu.VMEM((3, 2, 64, COLS), BF16),
+        pltpu.VMEM((3, 2, 64, COLS), BF16),
+        dma((4,)),
         *[dma((3,))] * 2,
         *[dma((2,))] * 2,
         *[dma((3, 4))] * 2,
@@ -475,21 +471,22 @@
         *[dma((3,))] * 2,
         *[dma((2, 4, 2))] * 8,
     ]
-    return pl.pallas_call(
+    iso_rows, env_rows = pl.pallas_call(
         kernel,
         out_shape=(
             jax.ShapeDtypeStruct((2, 16, COLS), BF16),
-            jax.ShapeDtypeStruct((2, 3, COLS, 64), BF16),
+            jax.ShapeDtypeStruct((2, 3, 64, COLS), BF16),
         ),
-        in_specs=[smem, smem, anywhere, anywhere, vmem],
+        in_specs=[smem, smem, anywhere, anywhere, anywhere],
         out_specs=(vmem, vmem),
         scratch_shapes=scratch,
         compiler_params=pltpu.CompilerParams(
-            collective_id=0, has_side_effects=True, vmem_limit_bytes=40 * 2**20
+            collective_id=0, has_side_effects=True, vmem_limit_bytes=60 * 2**20
         ),
         cost_estimate=pl.CostEstimate(flops=8 * 10**9, bytes_accessed=8 * 2**20, transcendentals=0),
         name="dmrg_window",
-    )(shift_map, live_rows, wave_in, left_env, right_env)
+    )(shift_map.T, live_rows, wave_in, left_env, right_env.swapaxes(2, 3))
+    return iso_rows, env_rows.swapaxes(2, 3)
 
 
 def solution(mesh):

time: 102 us -> 98 us (0.961)
  local copies, waits for them, and re-layouts: 7.14 us -> 2.94 us
    unnamed x9 -> x2, local copies, waits for them, and re-layouts: 6.29 us -> 2.94 us
where the time goes in v2:
time: 98 us; the launch traced here: 97.7 us
  Pallas kernels  94.2 us (96%)
  local copies, waits for them, and re-layouts  2.94 us (3%)
    pallas_call x1, Pallas kernels, body(): pl.pallas_call(kernel, out_shape=(jax.ShapeDtypeStruct((2, 16, COLS), BF1...  94.2 us
    unnamed x2, local copies, waits for them, and re-layouts  2.94 us

profile of v2, /device:TPU:1, one launch (start us, length us, event | category | flops | bytes accessed | tf_op | source)
XLA Modules:
  0.0 97.7 jit_solution(7338337992573035174)
XLA Ops:
  0.6 94.2 %dmrg_window.1 = (bf16[2,16,256]{2,1,0:T(8,128)(2,1)}, bf16[2,3,64,256]{3,2,1,0:T(8,128)(2,1)}) custom-call(s32[16,48]{1,0:T(8,128)} %bitcast.5, s32[16]{0:T(128)} %live.1, bf16[2,1024,256]{2,1,0:T(8,128)(2,1)} %wave.1, bf16[2,3,1024,256]{3,2,1,0:T(8,128)(2,1)} %left.1, bf16[2,3,64,256]{3,2,1,0:T(8,128)(2,1)} %bitcast.4), custom_call_target="tpu_custom_call" | custom-call | flops 8000000000 | bytes 8388608 | tf_op jit(solution)/shard_map/dmrg_window/pallas_call | solution.py:474
  94.8 1.3 %copy.9 = bf16[2,16,256]{2,1,0:T(8,128)(2,1)} copy(bf16[2,16,256]{2,1,0:T(8,128)(2,1)} %get-tuple-element.8) | data formatting | bytes 32768
  96.1 1.6 %copy.10 = bf16[2,3,256,64]{2,3,1,0:T(8,128)(2,1)} copy(bf16[2,3,256,64]{2,3,1,0:T(8,128)(2,1)} %bitcast.3) | data formatting | bytes 393216

commit v3 on v2

v3 whole, which is shorter than its diff:
```python
import jax
import jax.numpy as jnp
from jax import lax
from jax.experimental import pallas as pl
from jax.experimental.pallas import tpu as pltpu
from jax.sharding import Mesh
from jax.sharding import PartitionSpec as P

STEPS = 8
NY, NX, NZ = 8, 4, 8
ROWS, COLS, HALF = 1024, 256, 128
CHUNKS = 2
CHUNK = HALF // CHUNKS
TERM = ("x", "z", "core")
STEP_SIZE = 0.15
EPSILON = 1e-06
MESH = pl.DeviceIdType.MESH
F32, BF16 = jnp.float32, jnp.bfloat16
FAR_FIRST = (4, 3, 5, 2, 6, 1, 7, 0)
X_FAR_FIRST = (2, 1, 3, 0)


def dot(a, b):
    return jnp.dot(a, b, preferred_element_type=F32)


def dot_over_rows(a, b):
    return lax.dot_general(a, b, (((0,), (0,)), ((), ())), preferred_element_type=F32)


def dot_over_columns(a, b):
    return lax.dot_general(a, b, (((1,), (1,)), ((), ())), preferred_element_type=F32)


def two_parts(a):
    high = a.astype(BF16)
    return high, (a - high.astype(F32)).astype(BF16)


def dot3(a, b):
    return dot(a[0], b[0]) + (dot(a[0], b[1]) + dot(a[1], b[0]))


def remote(src, dst, send, recv, to):
    return pltpu.make_async_remote_copy(
        src_ref=src, dst_ref=dst, send_sem=send, recv_sem=recv, device_id=to, device_id_type=MESH
    )


class Gather:
    def __init__(self, pos, blocks, sems):
        self.pos, self.blocks = pos, blocks
        self.y_send, self.y_recv, self.x_send, self.x_recv = sems
        self.half = lax.rem(pos["x"], 2)
        self.started = []

    def place(self, way, d, j, k, half):
        y, core = self.pos["sector"], self.pos["core"]
        step = d if way == 0 else NY - d
        sector = core if j == 0 else 1 - core
        index = 2 * lax.rem(y - step + 2 * NY, NY) + sector
        return self.blocks.at[index, pl.ds(pl.multiple_of(half * HALF + k * CHUNK, CHUNK), CHUNK), :]

    def to(self, way, j):
        y, x = self.pos["sector"], self.pos["x"]
        at = dict(self.pos)
        if way is not None:
            at["sector"] = lax.rem(y + (1 if way == 0 else NY - 1), NY)
        if j is not None:
            at["x"] = lax.rem(x + (1 if j == 0 else NX - 1), NX)
        return at

    def neighbours(self):
        ways, sides = (0, 1, None), (0, 1, None)
        return [self.to(w, j) for w in ways for j in sides if w is not None or j is not None]

    def go(self, copy):
        copy.start()
        self.started.append(copy)

    def along_y(self, source, way, d, j, k):
        at = (way, d, j, k)
        place = self.place(way, d, j, k, self.half)
        source = place if source is None else source
        self.go(remote(source, place, self.y_send.at[at], self.y_recv.at[at], self.to(way, None)))

    def along_x(self, way, d, j, k, ahead=False):
        at = (way, d if ahead else d - 1, j, k)
        block = self.place(way, d, j, k, self.half)
        self.go(remote(block, block, self.x_send.at[at], self.x_recv.at[at], self.to(way if ahead else None, j)))

    def start(self, j, source):
        for k in range(CHUNKS):
            for way in (0, 1):
                self.along_y(source.at[pl.ds(CHUNK * k, CHUNK), :], way, 0, j, k)

    def arrive(self, d):
        for j in (0, 1):
            for k in range(CHUNKS):
                for way in (0, 1):
                    if d == 4 and j != way:
                        continue
                    at = (way, d - 1, j, k)
                    block = self.place(way, d, j, k, self.half)
                    remote(block, block, self.y_send.at[at], self.y_recv.at[at], self.to(way, None)).wait_recv()
                    if d < 3 or (d == 3 and j == way):
                        self.along_y(None, way, d, j, k)
                        if d == 3:
                            self.along_x(way, d, j, k, ahead=True)
                    if d < 4:
                        self.along_x(way, d, j, k)

    def finish(self):
        for d in (1, 2, 3, 4):
            for j in (0, 1):
                for k in range(CHUNKS):
                    for way in (0, 1):
                        if d == 4 and j != way:
                            continue
                        at = (way, d - 1, j, k)
                        block = self.place(way, d, j, k, 1 - self.half)
                        remote(block, block, self.x_send.at[at], self.x_recv.at[at], self.to(None, j)).wait_recv()


def kernel(
    shift_in,
    live_in,
    wave,
    left,
    right,
    iso_out,
    env_out,
    shift,
    live,
    left_v,
    wave_v,
    wave_all,
    right_all,
    applied,
    sib_out,
    sib_in,
    sigma,
    x_out,
    x_own,
    x_in,
    z_out,
    z_own,
    z_in,
    total,
    u_high,
    u_low,
    root,
    inverse,
    iso,
    iso_all,
    front,
    e_out,
    e_in,
    e_own,
    ez_out,
    ez_in,
    env_v,
    local_sem,
    r_send,
    r_recv,
    sib_send,
    sib_recv,
    xs_send,
    xs_recv,
    zs_send,
    zs_recv,
    gz_send,
    gz_recv,
    gx_send,
    gx_recv,
    i_send,
    i_recv,
    e_send,
    e_recv,
    ez_send,
    ez_recv,
    *ring_sems,
):
    y, x, z, core = (lax.axis_index(a) for a in ("sector", "x", "z", "core"))
    pos = {"sector": y, "x": x, "z": z, "core": core}
    zb = lax.rem(z, 2)
    part = 2 * zb + core
    group = 4 * x + z // 2
    half = lax.rem(x, 2)
    other = 1 - core
    sibling = {**pos, "core": other}
    z_pair = {**pos, "z": z + 1 - 2 * zb}
    x_to = [{**pos, "x": lax.rem(x + dx, NX)} for dx in range(NX)]
    z_to = [{**pos, "z": lax.rem(z + dz, NZ)} for dz in range(NZ)]
    sectors = (core, other)
    waits = []

    def go(copy):
        copy.start()
        waits.append(copy)
        return copy

    part_row = pl.multiple_of(part * COLS, COLS)
    own_left = pltpu.make_async_copy(left, left_v, local_sem.at[0])
    own_wave = pltpu.make_async_copy(wave.at[core], wave_v, local_sem.at[1])
    own_block = pltpu.make_async_copy(
        wave.at[:, pl.ds(part_row, COLS), :], wave_all.at[pl.ds(2 * y, 2)], local_sem.at[2]
    )

    own_shift = pltpu.make_async_copy(shift_in, shift, local_sem.at[4])
    own_live = pltpu.make_async_copy(live_in, live, local_sem.at[5])
    first = Gather(pos, wave_all, ring_sems[:4])
    barrier = pltpu.get_barrier_semaphore()
    partners = first.neighbours() + [x_to[2]] + z_to[1:] + [sibling]
    for to in partners:
        pl.semaphore_signal(barrier, inc=1, device_id=to, device_id_type=MESH)
    pl.semaphore_wait(barrier, len(partners))

    send_row = pl.multiple_of(part * COLS + half * HALF, HALF)
    for j in (0, 1):
        first.start(j, wave.at[sectors[j], pl.ds(send_row, HALF), :])

    def right_rows(p):
        return right_all.at[:, :, pl.ds(pl.multiple_of(64 * p, 64), 64), :]

    mine = right_rows(part)
    own_right = pltpu.make_async_copy(right, mine, local_sem.at[3])
    go(remote(right, mine, r_send.at[1], r_recv.at[1], z_pair))
    go(remote(right, mine, r_send.at[0], r_recv.at[0], sibling))
    for copy in (own_shift, own_live, own_block, own_right, own_left, own_wave):
        copy.start()
    first.arrive(1)
    first.arrive(2)
    far = right_rows(2 * (1 - zb) + core)
    remote(far, far, r_send.at[1], r_recv.at[1], z_pair).wait_recv()
    go(remote(far, far, r_send.at[2], r_recv.at[2], sibling))
    first.arrive(3)
    near = right_rows(2 * zb + other)
    remote(near, near, r_send.at[0], r_recv.at[0], sibling).wait_recv()
    last = right_rows(2 * (1 - zb) + other)
    remote(last, last, r_send.at[2], r_recv.at[2], sibling).wait_recv()
    for copy in (own_shift, own_live, own_block, own_right, own_left, own_wave):
        copy.wait()
    first.arrive(4)
    first.finish()

    def row_order(dx):
        base = 256 * lax.rem(x + dx, NX)
        return [pl.ds(pl.multiple_of(base + 32 * lax.rem(z + dz, NZ), 32), 32) for dz in FAR_FIRST]

    def partial_sum(s, dx):
        pieces = row_order(dx)
        acc = jnp.zeros((256, COLS), F32)
        for term in range(3):
            rows = jnp.concatenate([left_v[s, term, p, :] for p in pieces], axis=0)
            acc = acc + dot(rows, applied[s, term])
        return acc

    def apply(s):
        for term in range(3):
            source = shift[2 * y + s, 3 * group + term]
            applied[s, term] = dot_over_columns(wave_all[source], right_all[s, term]).astype(BF16)

    def from_sibling_sum(q):
        h = pl.ds(512 * q, 512)
        return remote(sib_out.at[h], sib_in.at[h], sib_send.at[q], sib_recv.at[q], sibling)

    apply(other)
    for i, dx in enumerate(X_FAR_FIRST):
        sib_out[256 * i : 256 * (i + 1), :] = partial_sum(other, dx).astype(BF16)
        if i % 2 == 1:
            go(from_sibling_sum(i // 2))
    apply(core)
    for i in (0, 1):
        sigma[256 * i : 256 * (i + 1), :] = partial_sum(core, X_FAR_FIRST[i])

    for i, dx in enumerate(X_FAR_FIRST):
        if i % 2 == 0:
            from_sibling_sum(i // 2).wait_recv()
        if i < 2:
            acc = sigma[256 * i : 256 * (i + 1), :]
        else:
            acc = partial_sum(core, dx)
        acc = acc + sib_in[256 * i : 256 * (i + 1), :].astype(F32)
        if dx == 0:
            x_own[...] = acc
            continue
        x_out[dx - 1] = acc.astype(BF16)
        for g in range(4):
            h = pl.ds(64 * g, 64)
            go(
                remote(
                    x_out.at[dx - 1, h],
                    x_in.at[dx - 1, h],
                    xs_send.at[dx - 1, g],
                    xs_recv.at[dx - 1, g],
                    x_to[dx],
                )
            )
    for g in range(4):
        rows = slice(64 * g, 64 * (g + 1))
        acc = x_own[rows, :]
        for dx in (1, 2, 3):
            h = pl.ds(64 * g, 64)
            remote(
                x_out.at[dx - 1, h], x_in.at[dx - 1, h], xs_send.at[dx - 1, g], xs_recv.at[dx - 1, g], x_to[dx]
            ).wait_recv()
            acc = acc + x_in[dx - 1, rows, :].astype(F32)
        for i in (2 * g, 2 * g + 1):
            piece = acc[32 * (i % 2) : 32 * (i % 2 + 1), :]
            if FAR_FIRST[i]:
                z_out[i] = piece.astype(BF16)
                go(remote(z_out.at[i], z_in.at[i], zs_send.at[i], zs_recv.at[i], z_to[FAR_FIRST[i]]))
            else:
                z_own[...] = piece
    acc = z_own[...]
    for i in range(7):
        remote(z_out.at[i], z_in.at[i], zs_send.at[i], zs_recv.at[i], z_to[FAR_FIRST[i]]).wait_recv()
        acc = acc + z_in[i].astype(F32)

    def piece_at(dx, dz):
        at = 256 * lax.rem(x + NX - dx, NX) + 32 * lax.rem(z + NZ - dz, NZ)
        return total.at[pl.ds(pl.multiple_of(at, 32), 32)]

    own_piece = piece_at(0, 0)
    own_piece[...] = acc.astype(BF16)
    for i in range(7):
        go(remote(own_piece, own_piece, gz_send.at[i], gz_recv.at[i], z_to[FAR_FIRST[i]]))
    for i in range(7, -1, -1):
        piece = piece_at(0, FAR_FIRST[i])
        if i < 7:
            remote(piece, piece, gz_send.at[i], gz_recv.at[i], z_to[FAR_FIRST[i]]).wait_recv()
        for dx in (2, 1, 3):
            go(remote(piece, piece, gx_send.at[dx - 1, i], gx_recv.at[dx - 1, i], x_to[dx]))

    limit = live[2 * y + core]
    gram = jnp.zeros((COLS, COLS), F32)
    cross = jnp.zeros((COLS, COLS), F32)
    for dx in (0, 1, 3, 2):
        if dx:
            for i in range(7, -1, -1):
                piece = piece_at(dx, FAR_FIRST[i])
                remote(piece, piece, gx_send.at[dx - 1, i], gx_recv.at[dx - 1, i], x_to[dx]).wait_recv()
        base = pl.multiple_of(256 * lax.rem(x + NX - dx, NX), 256)
        rows = pl.ds(base, 256)
        row_ids = base + lax.broadcasted_iota(jnp.int32, (256, COLS), 0)
        value = wave_v[rows, :].astype(F32) - STEP_SIZE * total[rows, :].astype(F32)
        high, low = two_parts(jnp.where(row_ids < limit, value, 0.0))
        u_high[rows, :] = high
        u_low[rows, :] = low
        gram = gram + dot_over_rows(high, high)
        cross = cross + dot_over_rows(high, low)
    gram = gram + (cross + cross.T)
    diagonal = lax.broadcasted_iota(jnp.int32, (COLS, COLS), 0) == lax.broadcasted_iota(jnp.int32, (COLS, COLS), 1)
    trace = jnp.sum(jnp.where(diagonal, gram, 0.0), keepdims=True) + EPSILON
    three_halves = jnp.where(diagonal, 1.5, 0.0)
    y0 = gram / trace
    factor = three_halves - 0.5 * y0
    root[...] = dot3(two_parts(y0), two_parts(factor))
    inverse[...] = factor

    def newton_schulz(_, carry):
        y_parts, z_parts = two_parts(root[...]), two_parts(inverse[...])
        f_parts = two_parts(three_halves - 0.5 * dot3(z_parts, y_parts))
        root[...] = dot3(y_parts, f_parts)
        inverse[...] = dot3(f_parts, z_parts)
        return carry

    lax.fori_loop(0, STEPS - 2, newton_schulz, 0)
    y_parts, z_parts = two_parts(root[...]), two_parts(inverse[...])
    f_parts = two_parts(three_halves - 0.5 * dot3(z_parts, y_parts))
    z_parts = two_parts(dot3(f_parts, z_parts))
    scale = jnp.sqrt(ROWS / trace)

    second = Gather(pos, iso_all, ring_sems[4:])

    def make_rows(b, c, h):
        rows = pl.ds(pl.multiple_of(512 * b + 256 * c + HALF * h, HALF), HALF)
        a = (u_high[rows, :], u_low[rows, :])
        iso[core, b, c, h] = (dot3(a, z_parts) * scale).astype(BF16)

    def swap(n, s):
        asked = 1 - s
        if n == 0:
            block = iso.at[s, zb, asked, half]
        elif n == 1:
            block = iso.at[s, zb, s, half]
        elif n == 2:
            block = iso.at[s, zb, :, 1 - half]
        else:
            block = iso.at[s, 1 - zb]
        return remote(block, block, i_send.at[n], i_recv.at[n], sibling)

    make_rows(zb, core, half)
    second.start(0, iso.at[core, zb, core, half])
    make_rows(zb, other, half)
    go(swap(0, core))
    for c in (core, other):
        make_rows(zb, c, 1 - half)
    for c in (0, 1):
        for h in (0, 1):
            make_rows(1 - zb, c, h)
    swap(0, other).wait_recv()
    second.start(1, iso.at[other, zb, core, half])
    for n in (1, 2, 3):
        go(swap(n, core))

    def project(s):
        rows = iso[s].reshape(ROWS, COLS)
        for term in range(3):
            front[s, term] = dot_over_rows(left_v[s, term], rows).astype(BF16)

    project(core)
    second.arrive(1)
    for n in (1, 2, 3):
        swap(n, other).wait_recv()
    project(other)
    second.arrive(2)
    own_rows = iso.at[:, x // 2, lax.rem(x, 2), z // 4, pl.ds(pl.multiple_of(32 * lax.rem(z, 4) + 16 * core, 16), 16)]
    out_iso = pltpu.make_async_copy(own_rows, iso_out, local_sem.at[6])
    out_iso.start()
    for s in (0, 1):
        iso_all[2 * y + s] = iso[s, zb, core].reshape(COLS, COLS)
    second.arrive(3)
    second.arrive(4)
    second.finish()

    for term in range(3):
        for s in (0, 1):
            source = shift[2 * y + s, 3 * group + term]
            value = dot_over_rows(iso_all[source], front[s, term]) * (1 / 32)
            for a in (0, 1):
                one, two = value[128 * a : 128 * a + 64, :], value[128 * a + 64 : 128 * (a + 1), :]
                e_own[a, term, s] = jnp.where(core == 0, one, two)
                e_out[term, a, s] = jnp.where(core == 0, two, one).astype(BF16)
        go(remote(e_out.at[term], e_in.at[term], e_send.at[term], e_recv.at[term], sibling))
    for term in range(3):
        remote(e_out.at[term], e_in.at[term], e_send.at[term], e_recv.at[term], sibling).wait_recv()
        ez_out[term] = (e_own[1 - zb, term] + e_in[term, 1 - zb].astype(F32)).astype(BF16)
        go(remote(ez_out.at[term], ez_in.at[term], ez_send.at[term], ez_recv.at[term], z_pair))
    outs = [out_iso]
    for term in range(3):
        kept = e_own[zb, term] + e_in[term, zb].astype(F32)
        remote(ez_out.at[term], ez_in.at[term], ez_send.at[term], ez_recv.at[term], z_pair).wait_recv()
        kept = kept + ez_in[term].astype(F32)
        env_v[term] = kept.astype(BF16)
        out_env = pltpu.make_async_copy(env_v.at[term], env_out.at[:, term], local_sem.at[7 + term])
        out_env.start()
        outs.append(out_env)

    for copy in waits + first.started + second.started:
        copy.wait_send()
    for copy in outs:
        copy.wait()


def body(wave_in, left_env, right_env, shift_map, live_rows):
    dma = pltpu.SemaphoreType.DMA
    anywhere = pl.BlockSpec(memory_space=pl.ANY)
    scratch = [
        pltpu.SMEM((16, 48), jnp.int32),
        pltpu.SMEM((16,), jnp.int32),
        pltpu.VMEM((2, 3, ROWS, COLS), BF16),
        pltpu.VMEM((ROWS, COLS), BF16),
        pltpu.VMEM((16, COLS, COLS), BF16),
        pltpu.VMEM((2, 3, COLS, COLS), BF16),
        pltpu.VMEM((2, 3, COLS, COLS), BF16),
        pltpu.VMEM((ROWS, COLS), BF16),
        pltpu.VMEM((ROWS, COLS), BF16),
        pltpu.VMEM((512, COLS), F32),
        pltpu.VMEM((3, 256, COLS), BF16),
        pltpu.VMEM((256, COLS), F32),
        pltpu.VMEM((3, 256, COLS), BF16),
        pltpu.VMEM((7, 32, COLS), BF16),
        pltpu.VMEM((32, COLS), F32),
        pltpu.VMEM((7, 32, COLS), BF16),
        pltpu.VMEM((ROWS, COLS), BF16),
        pltpu.VMEM((ROWS, COLS), BF16),
        pltpu.VMEM((ROWS, COLS), BF16),
        pltpu.VMEM((COLS, COLS), F32),
        pltpu.VMEM((COLS, COLS), F32),
        pltpu.VMEM((2, 2, 2, 2, HALF, COLS), BF16),
        pltpu.VMEM((16, COLS, COLS), BF16),
        pltpu.VMEM((2, 3, COLS, COLS), BF16),
        pltpu.VMEM((3, 2, 2, 64, COLS), BF16),
        pltpu.VMEM((3, 2, 2, 64, COLS), BF16),
        pltpu.VMEM((2, 3, 2, 64, COLS), F32),
        pltpu.VMEM((3, 2, 64, COLS), BF16),
        pltpu.VMEM((3, 2, 64, COLS), BF16),
        pltpu.VMEM((3, 2, 64, COLS), BF16),
        dma((10,)),
        *[dma((3,))] * 2,
        *[dma((2,))] * 2,
        *[dma((3, 4))] * 2,
        *[dma((7,))] * 2,
        *[dma((7,))] * 2,
        *[dma((3, 8))] * 2,
        *[dma((4,))] * 2,
        *[dma((3,))] * 2,
        *[dma((3,))] * 2,
        *[dma((2, 4, 2, CHUNKS))] * 8,
    ]
    iso_rows, env_rows = pl.pallas_call(
        kernel,
        out_shape=(
            jax.ShapeDtypeStruct((2, 16, COLS), BF16),
            jax.ShapeDtypeStruct((2, 3, 64, COLS), BF16),
        ),
        in_specs=[anywhere] * 5,
        out_specs=(anywhere, anywhere),
        scratch_shapes=scratch,
        compiler_params=pltpu.CompilerParams(
            collective_id=0, has_side_effects=True, vmem_limit_bytes=60 * 2**20
        ),
        cost_estimate=pl.CostEstimate(flops=8 * 10**9, bytes_accessed=8 * 2**20, transcendentals=0),
        name="dmrg_window",
    )(shift_map.T, live_rows, wave_in, left_env, right_env.swapaxes(2, 3))
    return iso_rows, env_rows.swapaxes(2, 3)


def solution(mesh):
    split = Mesh(mesh.devices.reshape(NY, NX, NZ, 2), ("sector", *TERM))
    return jax.shard_map(
        body,
        mesh=split,
        in_specs=(
            P("sector", None, None),
            P("sector", TERM, None, None),
            P("sector", TERM, None, None),
            P(),
            P(),
        ),
        out_specs=(P("sector", TERM, None), P("sector", TERM, None, None)),
        check_vma=False,
    )
```

time: 98 us -> 93.8 us (0.957)
  Pallas kernels: 94.2 us -> 90 us
    pallas_call x1, Pallas kernels: 94.2 us -> 90 us  [body(): pl.pallas_call(kernel, out_shape=(jax.ShapeDtypeStruct((2, 16, COLS), BF1...]
where the time goes in v3:
time: 93.8 us; the launch traced here: 93.6 us
  Pallas kernels  90 us (96%)
  local copies, waits for them, and re-layouts  2.94 us (3%)
    pallas_call x1, Pallas kernels, body(): pl.pallas_call(kernel, out_shape=(jax.ShapeDtypeStruct((2, 16, COLS), BF1...  90 us
    unnamed x2, local copies, waits for them, and re-layouts  2.94 us

profile of v3, /device:TPU:1, one launch (start us, length us, event | category | flops | bytes accessed | tf_op | source)
XLA Modules:
  0.0 93.6 jit_solution(3712066323842751385)
XLA Ops:
  0.6 90.0 %dmrg_window.1 = (bf16[2,16,256]{2,1,0:T(8,128)(2,1)}, bf16[2,3,64,256]{3,2,1,0:T(8,128)(2,1)}) custom-call(s32[16,48]{1,0:T(8,128)} %bitcast.5, s32[16]{0:T(128)} %live_in.1, bf16[2,1024,256]{2,1,0:T(8,128)(2,1)} %wave.1, bf16[2,3,1024,256]{3,2,1,0:T(8,128)(2,1)} %left.1, bf16[2,3,64,256]{3,2,1,0:T(8,128)(2,1)} %bitcast.4), custom_call_target="tpu_custom_call" | custom-call | flops 8000000000 | bytes 8388608 | tf_op jit(solution)/shard_map/dmrg_window/pallas_call | solution.py:503
  90.7 1.3 %copy.9 = bf16[2,16,256]{2,1,0:T(8,128)(2,1)} copy(bf16[2,16,256]{2,1,0:T(8,128)(2,1)} %get-tuple-element.8) | data formatting | bytes 32768
  92.0 1.6 %copy.10 = bf16[2,3,256,64]{2,3,1,0:T(8,128)(2,1)} copy(bf16[2,3,256,64]{2,3,1,0:T(8,128)(2,1)} %bitcast.3) | data formatting | bytes 393216

commit v4 on v3

--- a/solution.py
+++ b/solution.py
@@ -48,8 +48,8 @@
 
 
 class Gather:
-    def __init__(self, pos, blocks, sems):
-        self.pos, self.blocks = pos, blocks
+    def __init__(self, pos, chunk_at, sems):
+        self.pos, self.chunk_at = pos, chunk_at
         self.y_send, self.y_recv, self.x_send, self.x_recv = sems
         self.half = lax.rem(pos["x"], 2)
         self.started = []
@@ -59,7 +59,7 @@
         step = d if way == 0 else NY - d
         sector = core if j == 0 else 1 - core
         index = 2 * lax.rem(y - step + 2 * NY, NY) + sector
-        return self.blocks.at[index, pl.ds(pl.multiple_of(half * HALF + k * CHUNK, CHUNK), CHUNK), :]
+        return self.chunk_at(index, half, k)
 
     def to(self, way, j):
         y, x = self.pos["sector"], self.pos["x"]
@@ -92,7 +92,7 @@
     def start(self, j, source):
         for k in range(CHUNKS):
             for way in (0, 1):
-                self.along_y(source.at[pl.ds(CHUNK * k, CHUNK), :], way, 0, j, k)
+                self.along_y(source(k), way, 0, j, k)
 
     def arrive(self, d):
         for j in (0, 1):
@@ -146,6 +146,7 @@
     z_out,
     z_own,
     z_in,
+    far_in,
     total,
     u_high,
     u_low,
@@ -157,8 +158,6 @@
     e_out,
     e_in,
     e_own,
-    ez_out,
-    ez_in,
     env_v,
     local_sem,
     r_send,
@@ -177,8 +176,10 @@
     i_recv,
     e_send,
     e_recv,
-    ez_send,
-    ez_recv,
+    fs_send,
+    fs_recv,
+    f_send,
+    f_recv,
     *ring_sems,
 ):
     y, x, z, core = (lax.axis_index(a) for a in ("sector", "x", "z", "core"))
@@ -209,16 +210,21 @@
 
     own_shift = pltpu.make_async_copy(shift_in, shift, local_sem.at[4])
     own_live = pltpu.make_async_copy(live_in, live, local_sem.at[5])
-    first = Gather(pos, wave_all, ring_sems[:4])
+
+    def wave_chunk(index, h, k):
+        return wave_all.at[index, pl.ds(pl.multiple_of(h * HALF + k * CHUNK, CHUNK), CHUNK), :]
+
+    first = Gather(pos, wave_chunk, ring_sems[:4])
     barrier = pltpu.get_barrier_semaphore()
-    partners = first.neighbours() + [x_to[2]] + z_to[1:] + [sibling]
+    far_to = [{**x_to[dx], "z": z_to[4]["z"]} for dx in range(NX)]
+    partners = first.neighbours() + [sibling, x_to[2]] + z_to[1:] + far_to[1:]
     for to in partners:
         pl.semaphore_signal(barrier, inc=1, device_id=to, device_id_type=MESH)
     pl.semaphore_wait(barrier, len(partners))
 
-    send_row = pl.multiple_of(part * COLS + half * HALF, HALF)
+    send_row = part * COLS + half * HALF
     for j in (0, 1):
-        first.start(j, wave.at[sectors[j], pl.ds(send_row, HALF), :])
+        first.start(j, lambda k: wave.at[sectors[j], pl.ds(pl.multiple_of(send_row + CHUNK * k, CHUNK), CHUNK), :])
 
     def right_rows(p):
         return right_all.at[:, :, pl.ds(pl.multiple_of(64 * p, 64), 64), :]
@@ -274,6 +280,17 @@
     for i in (0, 1):
         sigma[256 * i : 256 * (i + 1), :] = partial_sum(core, X_FAR_FIRST[i])
 
+    def to_far(dx):
+        return remote(
+            x_out.at[dx - 1, pl.ds(0, 32)], far_in.at[dx - 1], fs_send.at[dx - 1], fs_recv.at[dx - 1], far_to[dx]
+        )
+
+    def to_x(dx, g):
+        h = pl.ds(32, 32) if g == 0 else pl.ds(64 * g, 64)
+        return remote(
+            x_out.at[dx - 1, h], x_in.at[dx - 1, h], xs_send.at[dx - 1, g], xs_recv.at[dx - 1, g], x_to[dx]
+        )
+
     for i, dx in enumerate(X_FAR_FIRST):
         if i % 2 == 0:
             from_sibling_sum(i // 2).wait_recv()
@@ -284,30 +301,22 @@
         acc = acc + sib_in[256 * i : 256 * (i + 1), :].astype(F32)
         if dx == 0:
             x_own[...] = acc
+            z_out[0] = acc[:32, :].astype(BF16)
+            go(remote(z_out.at[0], z_in.at[0], zs_send.at[0], zs_recv.at[0], z_to[4]))
             continue
         x_out[dx - 1] = acc.astype(BF16)
+        go(to_far(dx))
         for g in range(4):
-            h = pl.ds(64 * g, 64)
-            go(
-                remote(
-                    x_out.at[dx - 1, h],
-                    x_in.at[dx - 1, h],
-                    xs_send.at[dx - 1, g],
-                    xs_recv.at[dx - 1, g],
-                    x_to[dx],
-                )
-            )
+            go(to_x(dx, g))
     for g in range(4):
-        rows = slice(64 * g, 64 * (g + 1))
+        slots = range(max(1, 2 * g), 2 * g + 2)
+        rows = slice(32 * slots[0], 64 * (g + 1))
         acc = x_own[rows, :]
         for dx in (1, 2, 3):
-            h = pl.ds(64 * g, 64)
-            remote(
-                x_out.at[dx - 1, h], x_in.at[dx - 1, h], xs_send.at[dx - 1, g], xs_recv.at[dx - 1, g], x_to[dx]
-            ).wait_recv()
+            to_x(dx, g).wait_recv()
             acc = acc + x_in[dx - 1, rows, :].astype(F32)
-        for i in (2 * g, 2 * g + 1):
-            piece = acc[32 * (i % 2) : 32 * (i % 2 + 1), :]
+        for i in slots:
+            piece = acc[32 * (i - slots[0]) : 32 * (i - slots[0] + 1), :]
             if FAR_FIRST[i]:
                 z_out[i] = piece.astype(BF16)
                 go(remote(z_out.at[i], z_in.at[i], zs_send.at[i], zs_recv.at[i], z_to[FAR_FIRST[i]]))
@@ -317,6 +326,9 @@
     for i in range(7):
         remote(z_out.at[i], z_in.at[i], zs_send.at[i], zs_recv.at[i], z_to[FAR_FIRST[i]]).wait_recv()
         acc = acc + z_in[i].astype(F32)
+    for dx in (1, 2, 3):
+        to_far(dx).wait_recv()
+        acc = acc + far_in[dx - 1].astype(F32)
 
     def piece_at(dx, dz):
         at = 256 * lax.rem(x + NX - dx, NX) + 32 * lax.rem(z + NZ - dz, NZ)
@@ -326,10 +338,15 @@
     own_piece[...] = acc.astype(BF16)
     for i in range(7):
         go(remote(own_piece, own_piece, gz_send.at[i], gz_recv.at[i], z_to[FAR_FIRST[i]]))
+        if i == 0:
+            for dx in (2, 1, 3):
+                go(remote(own_piece, own_piece, gx_send.at[dx - 1, 0], gx_recv.at[dx - 1, 0], far_to[dx]))
     for i in range(7, -1, -1):
         piece = piece_at(0, FAR_FIRST[i])
         if i < 7:
             remote(piece, piece, gz_send.at[i], gz_recv.at[i], z_to[FAR_FIRST[i]]).wait_recv()
+        if i == 0:
+            continue
         for dx in (2, 1, 3):
             go(remote(piece, piece, gx_send.at[dx - 1, i], gx_recv.at[dx - 1, i], x_to[dx]))
 
@@ -372,79 +389,77 @@
     z_parts = two_parts(dot3(f_parts, z_parts))
     scale = jnp.sqrt(ROWS / trace)
 
-    second = Gather(pos, iso_all, ring_sems[4:])
-
-    def make_rows(b, c, h):
-        rows = pl.ds(pl.multiple_of(512 * b + 256 * c + HALF * h, HALF), HALF)
-        a = (u_high[rows, :], u_low[rows, :])
-        iso[core, b, c, h] = (dot3(a, z_parts) * scale).astype(BF16)
+    columns = pl.ds(pl.multiple_of(128 * zb, 128), 128)
+    second = Gather(pos, lambda index, h, k: iso_all.at[index, h, k], ring_sems[4:])
+
+    def make_rows(b, c):
+        for h in (0, 1):
+            rows = pl.ds(pl.multiple_of(512 * b + 256 * c + HALF * h, HALF), HALF)
+            a = (u_high[rows, :], u_low[rows, :])
+            iso[core, b, c, h] = (dot3(a, z_parts) * scale).astype(BF16)
 
     def swap(n, s):
-        asked = 1 - s
-        if n == 0:
-            block = iso.at[s, zb, asked, half]
-        elif n == 1:
-            block = iso.at[s, zb, s, half]
-        elif n == 2:
-            block = iso.at[s, zb, :, 1 - half]
-        else:
-            block = iso.at[s, 1 - zb]
+        block = (iso.at[s, half, 1 - s], iso.at[s, half, s], iso.at[s, 1 - half])[n]
         return remote(block, block, i_send.at[n], i_recv.at[n], sibling)
 
-    make_rows(zb, core, half)
-    second.start(0, iso.at[core, zb, core, half])
-    make_rows(zb, other, half)
+    make_rows(half, core)
+    second.start(0, lambda k: iso.at[core, half, core, k, :, columns])
+    make_rows(half, other)
     go(swap(0, core))
-    for c in (core, other):
-        make_rows(zb, c, 1 - half)
     for c in (0, 1):
-        for h in (0, 1):
-            make_rows(1 - zb, c, h)
+        make_rows(1 - half, c)
+    go(swap(1, core))
+    go(swap(2, core))
     swap(0, other).wait_recv()
-    second.start(1, iso.at[other, zb, core, half])
-    for n in (1, 2, 3):
-        go(swap(n, core))
-
-    def project(s):
-        rows = iso[s].reshape(ROWS, COLS)
+    second.start(1, lambda k: iso.at[other, half, core, k, :, columns])
+
+    def to_pair(n, term):
+        block = front.at[sectors[n], term, zb]
+        return remote(block, block, f_send.at[n, term], f_recv.at[n, term], z_pair)
+
+    def project(n):
+        rows = iso[sectors[n]].reshape(ROWS, COLS)
         for term in range(3):
-            front[s, term] = dot_over_rows(left_v[s, term], rows).astype(BF16)
-
-    project(core)
+            front[sectors[n], term, zb] = dot_over_rows(left_v[sectors[n], term], rows).astype(BF16)
+            go(to_pair(n, term))
+
+    project(0)
     second.arrive(1)
-    for n in (1, 2, 3):
+    for n in (1, 2):
         swap(n, other).wait_recv()
-    project(other)
+    project(1)
     second.arrive(2)
     own_rows = iso.at[:, x // 2, lax.rem(x, 2), z // 4, pl.ds(pl.multiple_of(32 * lax.rem(z, 4) + 16 * core, 16), 16)]
     out_iso = pltpu.make_async_copy(own_rows, iso_out, local_sem.at[6])
+    own_block = pltpu.make_async_copy(
+        iso.at[:, :, core, :, :, columns], iso_all.at[pl.ds(2 * y, 2)], local_sem.at[7]
+    )
     out_iso.start()
-    for s in (0, 1):
-        iso_all[2 * y + s] = iso[s, zb, core].reshape(COLS, COLS)
+    own_block.start()
     second.arrive(3)
     second.arrive(4)
     second.finish()
-
-    for term in range(3):
-        for s in (0, 1):
+    own_block.wait()
+
+    def to_sibling(n):
+        s = sectors[n]
+        return remote(e_out.at[s], e_in.at[s], e_send.at[n], e_recv.at[n], sibling)
+
+    for n, s in enumerate(sectors):
+        for term in range(3):
+            to_pair(n, term).wait_recv()
             source = shift[2 * y + s, 3 * group + term]
-            value = dot_over_rows(iso_all[source], front[s, term]) * (1 / 32)
-            for a in (0, 1):
-                one, two = value[128 * a : 128 * a + 64, :], value[128 * a + 64 : 128 * (a + 1), :]
-                e_own[a, term, s] = jnp.where(core == 0, one, two)
-                e_out[term, a, s] = jnp.where(core == 0, two, one).astype(BF16)
-        go(remote(e_out.at[term], e_in.at[term], e_send.at[term], e_recv.at[term], sibling))
-    for term in range(3):
-        remote(e_out.at[term], e_in.at[term], e_send.at[term], e_recv.at[term], sibling).wait_recv()
-        ez_out[term] = (e_own[1 - zb, term] + e_in[term, 1 - zb].astype(F32)).astype(BF16)
-        go(remote(ez_out.at[term], ez_in.at[term], ez_send.at[term], ez_recv.at[term], z_pair))
+            rows = iso_all[source].reshape(512, 128)
+            value = dot_over_rows(rows, front[s, term].reshape(512, COLS)) * (1 / 32)
+            e_own[s, term] = jnp.where(core == 0, value[:64, :], value[64:, :])
+            e_out[s, term] = jnp.where(core == 0, value[64:, :], value[:64, :]).astype(BF16)
+        go(to_sibling(n))
     outs = [out_iso]
-    for term in range(3):
-        kept = e_own[zb, term] + e_in[term, zb].astype(F32)
-        remote(ez_out.at[term], ez_in.at[term], ez_send.at[term], ez_recv.at[term], z_pair).wait_recv()
-        kept = kept + ez_in[term].astype(F32)
-        env_v[term] = kept.astype(BF16)
-        out_env = pltpu.make_async_copy(env_v.at[term], env_out.at[:, term], local_sem.at[7 + term])
+    for n in (0, 1):
+        s = sectors[1 - n]
+        remote(e_out.at[s], e_in.at[s], e_send.at[n], e_recv.at[n], sibling).wait_recv()
+        env_v[s] = (e_own[s] + e_in[s].astype(F32)).astype(BF16)
+        out_env = pltpu.make_async_copy(env_v.at[s], env_out.at[s], local_sem.at[8 + n])
         out_env.start()
         outs.append(out_env)
 
@@ -474,20 +489,19 @@
         pltpu.VMEM((7, 32, COLS), BF16),
         pltpu.VMEM((32, COLS), F32),
         pltpu.VMEM((7, 32, COLS), BF16),
+        pltpu.VMEM((3, 32, COLS), BF16),
         pltpu.VMEM((ROWS, COLS), BF16),
         pltpu.VMEM((ROWS, COLS), BF16),
         pltpu.VMEM((ROWS, COLS), BF16),
         pltpu.VMEM((COLS, COLS), F32),
         pltpu.VMEM((COLS, COLS), F32),
         pltpu.VMEM((2, 2, 2, 2, HALF, COLS), BF16),
-        pltpu.VMEM((16, COLS, COLS), BF16),
-        pltpu.VMEM((2, 3, COLS, COLS), BF16),
-        pltpu.VMEM((3, 2, 2, 64, COLS), BF16),
-        pltpu.VMEM((3, 2, 2, 64, COLS), BF16),
-        pltpu.VMEM((2, 3, 2, 64, COLS), F32),
-        pltpu.VMEM((3, 2, 64, COLS), BF16),
-        pltpu.VMEM((3, 2, 64, COLS), BF16),
-        pltpu.VMEM((3, 2, 64, COLS), BF16),
+        pltpu.VMEM((16, 2, 2, HALF, 128), BF16),
+        pltpu.VMEM((2, 3, 2, COLS, COLS), BF16),
+        pltpu.VMEM((2, 3, 64, COLS), BF16),
+        pltpu.VMEM((2, 3, 64, COLS), BF16),
+        pltpu.VMEM((2, 3, 64, COLS), F32),
+        pltpu.VMEM((2, 3, 64, COLS), BF16),
         dma((10,)),
         *[dma((3,))] * 2,
         *[dma((2,))] * 2,
@@ -495,9 +509,10 @@
         *[dma((7,))] * 2,
         *[dma((7,))] * 2,
         *[dma((3, 8))] * 2,
-        *[dma((4,))] * 2,
         *[dma((3,))] * 2,
+        *[dma((2,))] * 2,
         *[dma((3,))] * 2,
+        *[dma((2, 3))] * 2,
         *[dma((2, 4, 2, CHUNKS))] * 8,
     ]
     iso_rows, env_rows = pl.pallas_call(

time: 93.8 us -> 94.2 us (level)
  no operation moved by 1% of the time
where the time goes in v4:
time: 94.2 us; the launch traced here: 94 us
  Pallas kernels  90.4 us (96%)
  local copies, waits for them, and re-layouts  2.94 us (3%)
    pallas_call x1, Pallas kernels, body(): pl.pallas_call(kernel, out_shape=(jax.ShapeDtypeStruct((2, 16, COLS), BF1...  90.4 us
    unnamed x2, local copies, waits for them, and re-layouts  2.94 us

profile of v4, /device:TPU:1, one launch (start us, length us, event | category | flops | bytes accessed | tf_op | source)
XLA Modules:
  0.0 94.0 jit_solution(11247294351063712888)
XLA Ops:
  0.6 90.4 %dmrg_window.1 = (bf16[2,16,256]{2,1,0:T(8,128)(2,1)}, bf16[2,3,64,256]{3,2,1,0:T(8,128)(2,1)}) custom-call(s32[16,48]{1,0:T(8,128)} %bitcast.5, s32[16]{0:T(128)} %live_in.1, bf16[2,1024,256]{2,1,0:T(8,128)(2,1)} %wave.1, bf16[2,3,1024,256]{3,2,1,0:T(8,128)(2,1)} %left.1, bf16[2,3,64,256]{3,2,1,0:T(8,128)(2,1)} %bitcast.4), custom_call_target="tpu_custom_call" | custom-call | flops 8000000000 | bytes 8388608 | tf_op jit(solution)/shard_map/dmrg_window/pallas_call | solution.py:518
  91.1 1.3 %copy.9 = bf16[2,16,256]{2,1,0:T(8,128)(2,1)} copy(bf16[2,16,256]{2,1,0:T(8,128)(2,1)} %get-tuple-element.8) | data formatting | bytes 32768
  92.4 1.6 %copy.10 = bf16[2,3,256,64]{2,3,1,0:T(8,128)(2,1)} copy(bf16[2,3,256,64]{2,3,1,0:T(8,128)(2,1)} %bitcast.3) | data formatting | bytes 393216

commit v5 on v4

--- a/solution.py
+++ b/solution.py
@@ -146,7 +146,7 @@
     z_out,
     z_own,
     z_in,
-    far_in,
+    left_pair,
     total,
     u_high,
     u_low,
@@ -176,8 +176,8 @@
     i_recv,
     e_send,
     e_recv,
-    fs_send,
-    fs_recv,
+    l_send,
+    l_recv,
     f_send,
     f_recv,
     *ring_sems,
@@ -216,8 +216,7 @@
 
     first = Gather(pos, wave_chunk, ring_sems[:4])
     barrier = pltpu.get_barrier_semaphore()
-    far_to = [{**x_to[dx], "z": z_to[4]["z"]} for dx in range(NX)]
-    partners = first.neighbours() + [sibling, x_to[2]] + z_to[1:] + far_to[1:]
+    partners = first.neighbours() + [sibling, x_to[2]] + z_to[1:]
     for to in partners:
         pl.semaphore_signal(barrier, inc=1, device_id=to, device_id_type=MESH)
     pl.semaphore_wait(barrier, len(partners))
@@ -236,6 +235,8 @@
     for copy in (own_shift, own_live, own_block, own_right, own_left, own_wave):
         copy.start()
     first.arrive(1)
+    pair_blocks = remote(left.at[other, pl.ds(1, 2)], left_pair, l_send.at[0], l_recv.at[0], z_pair)
+    go(pair_blocks)
     first.arrive(2)
     far = right_rows(2 * (1 - zb) + core)
     remote(far, far, r_send.at[1], r_recv.at[1], z_pair).wait_recv()
@@ -280,13 +281,8 @@
     for i in (0, 1):
         sigma[256 * i : 256 * (i + 1), :] = partial_sum(core, X_FAR_FIRST[i])
 
-    def to_far(dx):
-        return remote(
-            x_out.at[dx - 1, pl.ds(0, 32)], far_in.at[dx - 1], fs_send.at[dx - 1], fs_recv.at[dx - 1], far_to[dx]
-        )
-
     def to_x(dx, g):
-        h = pl.ds(32, 32) if g == 0 else pl.ds(64 * g, 64)
+        h = pl.ds(64 * g, 64)
         return remote(
             x_out.at[dx - 1, h], x_in.at[dx - 1, h], xs_send.at[dx - 1, g], xs_recv.at[dx - 1, g], x_to[dx]
         )
@@ -301,16 +297,13 @@
         acc = acc + sib_in[256 * i : 256 * (i + 1), :].astype(F32)
         if dx == 0:
             x_own[...] = acc
-            z_out[0] = acc[:32, :].astype(BF16)
-            go(remote(z_out.at[0], z_in.at[0], zs_send.at[0], zs_recv.at[0], z_to[4]))
             continue
         x_out[dx - 1] = acc.astype(BF16)
-        go(to_far(dx))
         for g in range(4):
             go(to_x(dx, g))
     for g in range(4):
-        slots = range(max(1, 2 * g), 2 * g + 2)
-        rows = slice(32 * slots[0], 64 * (g + 1))
+        slots = (2 * g, 2 * g + 1)
+        rows = slice(64 * g, 64 * (g + 1))
         acc = x_own[rows, :]
         for dx in (1, 2, 3):
             to_x(dx, g).wait_recv()
@@ -326,9 +319,6 @@
     for i in range(7):
         remote(z_out.at[i], z_in.at[i], zs_send.at[i], zs_recv.at[i], z_to[FAR_FIRST[i]]).wait_recv()
         acc = acc + z_in[i].astype(F32)
-    for dx in (1, 2, 3):
-        to_far(dx).wait_recv()
-        acc = acc + far_in[dx - 1].astype(F32)
 
     def piece_at(dx, dz):
         at = 256 * lax.rem(x + NX - dx, NX) + 32 * lax.rem(z + NZ - dz, NZ)
@@ -338,15 +328,10 @@
     own_piece[...] = acc.astype(BF16)
     for i in range(7):
         go(remote(own_piece, own_piece, gz_send.at[i], gz_recv.at[i], z_to[FAR_FIRST[i]]))
-        if i == 0:
-            for dx in (2, 1, 3):
-                go(remote(own_piece, own_piece, gx_send.at[dx - 1, 0], gx_recv.at[dx - 1, 0], far_to[dx]))
     for i in range(7, -1, -1):
         piece = piece_at(0, FAR_FIRST[i])
         if i < 7:
             remote(piece, piece, gz_send.at[i], gz_recv.at[i], z_to[FAR_FIRST[i]]).wait_recv()
-        if i == 0:
-            continue
         for dx in (2, 1, 3):
             go(remote(piece, piece, gx_send.at[dx - 1, i], gx_recv.at[dx - 1, i], x_to[dx]))
 
@@ -413,22 +398,30 @@
     swap(0, other).wait_recv()
     second.start(1, lambda k: iso.at[other, half, core, k, :, columns])
 
+    def swapped(n, term):
+        return n == 0 or term == 0
+
     def to_pair(n, term):
         block = front.at[sectors[n], term, zb]
         return remote(block, block, f_send.at[n, term], f_recv.at[n, term], z_pair)
 
-    def project(n):
+    def project(n, terms):
         rows = iso[sectors[n]].reshape(ROWS, COLS)
-        for term in range(3):
+        for term in terms:
             front[sectors[n], term, zb] = dot_over_rows(left_v[sectors[n], term], rows).astype(BF16)
-            go(to_pair(n, term))
-
-    project(0)
+            if swapped(n, term):
+                go(to_pair(n, term))
+            else:
+                front[sectors[n], term, 1 - zb] = dot_over_rows(left_pair[term - 1], rows).astype(BF16)
+
+    project(0, (0, 1, 2))
     second.arrive(1)
     for n in (1, 2):
         swap(n, other).wait_recv()
-    project(1)
+    project(1, (0,))
     second.arrive(2)
+    pair_blocks.wait_recv()
+    project(1, (1, 2))
     own_rows = iso.at[:, x // 2, lax.rem(x, 2), z // 4, pl.ds(pl.multiple_of(32 * lax.rem(z, 4) + 16 * core, 16), 16)]
     out_iso = pltpu.make_async_copy(own_rows, iso_out, local_sem.at[6])
     own_block = pltpu.make_async_copy(
@@ -447,7 +440,8 @@
 
     for n, s in enumerate(sectors):
         for term in range(3):
-            to_pair(n, term).wait_recv()
+            if swapped(n, term):
+                to_pair(n, term).wait_recv()
             source = shift[2 * y + s, 3 * group + term]
             rows = iso_all[source].reshape(512, 128)
             value = dot_over_rows(rows, front[s, term].reshape(512, COLS)) * (1 / 32)
@@ -489,7 +483,7 @@
         pltpu.VMEM((7, 32, COLS), BF16),
         pltpu.VMEM((32, COLS), F32),
         pltpu.VMEM((7, 32, COLS), BF16),
-        pltpu.VMEM((3, 32, COLS), BF16),
+        pltpu.VMEM((2, ROWS, COLS), BF16),
         pltpu.VMEM((ROWS, COLS), BF16),
         pltpu.VMEM((ROWS, COLS), BF16),
         pltpu.VMEM((ROWS, COLS), BF16),
@@ -511,7 +505,7 @@
         *[dma((3, 8))] * 2,
         *[dma((3,))] * 2,
         *[dma((2,))] * 2,
-        *[dma((3,))] * 2,
+        *[dma((1,))] * 2,
         *[dma((2, 3))] * 2,
         *[dma((2, 4, 2, CHUNKS))] * 8,
     ]

time: 94.2 us -> 89.8 us (0.953)
  Pallas kernels: 90.4 us -> 86.1 us
    pallas_call x1, Pallas kernels: 90.4 us -> 86.1 us  [body(): pl.pallas_call(kernel, out_shape=(jax.ShapeDtypeStruct((2, 16, COLS), BF1...]
where the time goes in v5:
time: 89.8 us; the launch traced here: 89.6 us
  Pallas kernels  86.1 us (96%)
  local copies, waits for them, and re-layouts  2.94 us (3%)
    pallas_call x1, Pallas kernels, body(): pl.pallas_call(kernel, out_shape=(jax.ShapeDtypeStruct((2, 16, COLS), BF1...  86.1 us
    unnamed x2, local copies, waits for them, and re-layouts  2.94 us

profile of v5, /device:TPU:1, one launch (start us, length us, event | category | flops | bytes accessed | tf_op | source)
XLA Modules:
  0.0 89.6 jit_solution(7641522815801082744)
XLA Ops:
  0.6 86.1 %dmrg_window.1 = (bf16[2,16,256]{2,1,0:T(8,128)(2,1)}, bf16[2,3,64,256]{3,2,1,0:T(8,128)(2,1)}) custom-call(s32[16,48]{1,0:T(8,128)} %bitcast.5, s32[16]{0:T(128)} %live_in.1, bf16[2,1024,256]{2,1,0:T(8,128)(2,1)} %wave.1, bf16[2,3,1024,256]{3,2,1,0:T(8,128)(2,1)} %left.1, bf16[2,3,64,256]{3,2,1,0:T(8,128)(2,1)} %bitcast.4), custom_call_target="tpu_custom_call" | custom-call | flops 8000000000 | bytes 8388608 | tf_op jit(solution)/shard_map/dmrg_window/pallas_call | solution.py:512
  86.7 1.3 %copy.9 = bf16[2,16,256]{2,1,0:T(8,128)(2,1)} copy(bf16[2,16,256]{2,1,0:T(8,128)(2,1)} %get-tuple-element.8) | data formatting | bytes 32768
  88.0 1.6 %copy.10 = bf16[2,3,256,64]{2,3,1,0:T(8,128)(2,1)} copy(bf16[2,3,256,64]{2,3,1,0:T(8,128)(2,1)} %bitcast.3) | data formatting | bytes 393216

commit v6 on v5

--- a/solution.py
+++ b/solution.py
@@ -71,8 +71,8 @@
         return at
 
     def neighbours(self):
-        ways, sides = (0, 1, None), (0, 1, None)
-        return [self.to(w, j) for w in ways for j in sides if w is not None or j is not None]
+        ways = ((0, None), (1, None), (None, 0), (None, 1), (0, 0), (0, 1), (1, 0), (1, 1))
+        return [self.to(way, j) for way, j in ways]
 
     def go(self, copy):
         copy.start()
@@ -88,6 +88,12 @@
         at = (way, d if ahead else d - 1, j, k)
         block = self.place(way, d, j, k, self.half)
         self.go(remote(block, block, self.x_send.at[at], self.x_recv.at[at], self.to(way if ahead else None, j)))
+
+    def wait_sends(self, keep=0):
+        count = len(self.started) - keep
+        for copy in self.started[:count]:
+            copy.wait_send()
+        del self.started[:count]
 
     def start(self, j, source):
         for k in range(CHUNKS):
@@ -419,6 +425,7 @@
     for n in (1, 2):
         swap(n, other).wait_recv()
     project(1, (0,))
+    first.wait_sends()
     second.arrive(2)
     pair_blocks.wait_recv()
     project(1, (1, 2))
@@ -429,14 +436,18 @@
     )
     out_iso.start()
     own_block.start()
+    for copy in waits:
+        copy.wait_send()
+    waits.clear()
     second.arrive(3)
+    second.wait_sends(keep=36)
     second.arrive(4)
     second.finish()
     own_block.wait()
 
-    def to_sibling(n):
-        s = sectors[n]
-        return remote(e_out.at[s], e_in.at[s], e_send.at[n], e_recv.at[n], sibling)
+    def to_sibling(n, s, term):
+        at = (s, term)
+        return remote(e_out.at[at], e_in.at[at], e_send.at[n, term], e_recv.at[n, term], sibling)
 
     for n, s in enumerate(sectors):
         for term in range(3):
@@ -447,17 +458,18 @@
             value = dot_over_rows(rows, front[s, term].reshape(512, COLS)) * (1 / 32)
             e_own[s, term] = jnp.where(core == 0, value[:64, :], value[64:, :])
             e_out[s, term] = jnp.where(core == 0, value[64:, :], value[:64, :]).astype(BF16)
-        go(to_sibling(n))
+            go(to_sibling(n, s, term))
     outs = [out_iso]
     for n in (0, 1):
         s = sectors[1 - n]
-        remote(e_out.at[s], e_in.at[s], e_send.at[n], e_recv.at[n], sibling).wait_recv()
+        for term in range(3):
+            to_sibling(n, s, term).wait_recv()
         env_v[s] = (e_own[s] + e_in[s].astype(F32)).astype(BF16)
         out_env = pltpu.make_async_copy(env_v.at[s], env_out.at[s], local_sem.at[8 + n])
         out_env.start()
         outs.append(out_env)
 
-    for copy in waits + first.started + second.started:
+    for copy in waits + second.started:
         copy.wait_send()
     for copy in outs:
         copy.wait()
@@ -504,7 +516,7 @@
         *[dma((7,))] * 2,
         *[dma((3, 8))] * 2,
         *[dma((3,))] * 2,
-        *[dma((2,))] * 2,
+        *[dma((2, 3))] * 2,
         *[dma((1,))] * 2,
         *[dma((2, 3))] * 2,
         *[dma((2, 4, 2, CHUNKS))] * 8,

time: 89.8 us -> 93.8 us (1.045)
  Pallas kernels: 86.1 us -> 90.1 us
    pallas_call x1, Pallas kernels: 86.1 us -> 90.1 us  [body(): pl.pallas_call(kernel, out_shape=(jax.ShapeDtypeStruct((2, 16, COLS), BF1...]
where the time goes in v6:
time: 93.8 us; the launch traced here: 93.6 us
  Pallas kernels  90.1 us (96%)
  local copies, waits for them, and re-layouts  2.94 us (3%)
    pallas_call x1, Pallas kernels, body(): pl.pallas_call(kernel, out_shape=(jax.ShapeDtypeStruct((2, 16, COLS), BF1...  90.1 us
    unnamed x2, local copies, waits for them, and re-layouts  2.94 us

profile of v6, /device:TPU:1, one launch (start us, length us, event | category | flops | bytes accessed | tf_op | source)
XLA Modules:
  0.0 93.6 jit_solution(8824889029957552184)
XLA Ops:
  0.6 90.1 %dmrg_window.1 = (bf16[2,16,256]{2,1,0:T(8,128)(2,1)}, bf16[2,3,64,256]{3,2,1,0:T(8,128)(2,1)}) custom-call(s32[16,48]{1,0:T(8,128)} %bitcast.5, s32[16]{0:T(128)} %live_in.1, bf16[2,1024,256]{2,1,0:T(8,128)(2,1)} %wave.1, bf16[2,3,1024,256]{3,2,1,0:T(8,128)(2,1)} %left.1, bf16[2,3,64,256]{3,2,1,0:T(8,128)(2,1)} %bitcast.4), custom_call_target="tpu_custom_call" | custom-call | flops 8000000000 | bytes 8388608 | tf_op jit(solution)/shard_map/dmrg_window/pallas_call | solution.py:524
  90.7 1.3 %copy.9 = bf16[2,16,256]{2,1,0:T(8,128)(2,1)} copy(bf16[2,16,256]{2,1,0:T(8,128)(2,1)} %get-tuple-element.8) | data formatting | bytes 32768
  92.0 1.6 %copy.10 = bf16[2,3,256,64]{2,3,1,0:T(8,128)(2,1)} copy(bf16[2,3,256,64]{2,3,1,0:T(8,128)(2,1)} %bitcast.3) | data formatting | bytes 393216

commit v7 on v5

--- a/solution.py
+++ b/solution.py
@@ -234,9 +234,9 @@
     go(remote(right, mine, r_send.at[0], r_recv.at[0], sibling))
     for copy in (own_shift, own_live, own_block, own_right, own_left, own_wave):
         copy.start()
-    first.arrive(1)
     pair_blocks = remote(left.at[other, pl.ds(1, 2)], left_pair, l_send.at[0], l_recv.at[0], z_pair)
     go(pair_blocks)
+    first.arrive(1)
     first.arrive(2)
     far = right_rows(2 * (1 - zb) + core)
     remote(far, far, r_send.at[1], r_recv.at[1], z_pair).wait_recv()

time: 89.8 us -> 89.7 us (level)
  no operation moved by 1% of the time
where the time goes in v7:
time: 89.7 us; the launch traced here: 89.5 us
  Pallas kernels  85.9 us (96%)
  local copies, waits for them, and re-layouts  2.94 us (3%)
    pallas_call x1, Pallas kernels, body(): pl.pallas_call(kernel, out_shape=(jax.ShapeDtypeStruct((2, 16, COLS), BF1...  85.9 us
    unnamed x2, local copies, waits for them, and re-layouts  2.94 us

profile of v7, /device:TPU:1, one launch (start us, length us, event | category | flops | bytes accessed | tf_op | source)
XLA Modules:
  0.0 89.5 jit_solution(12090957277455707922)
XLA Ops:
  0.6 85.9 %dmrg_window.1 = (bf16[2,16,256]{2,1,0:T(8,128)(2,1)}, bf16[2,3,64,256]{3,2,1,0:T(8,128)(2,1)}) custom-call(s32[16,48]{1,0:T(8,128)} %bitcast.5, s32[16]{0:T(128)} %live_in.1, bf16[2,1024,256]{2,1,0:T(8,128)(2,1)} %wave.1, bf16[2,3,1024,256]{3,2,1,0:T(8,128)(2,1)} %left.1, bf16[2,3,64,256]{3,2,1,0:T(8,128)(2,1)} %bitcast.4), custom_call_target="tpu_custom_call" | custom-call | flops 8000000000 | bytes 8388608 | tf_op jit(solution)/shard_map/dmrg_window/pallas_call | solution.py:512
  86.6 1.3 %copy.9 = bf16[2,16,256]{2,1,0:T(8,128)(2,1)} copy(bf16[2,16,256]{2,1,0:T(8,128)(2,1)} %get-tuple-element.8) | data formatting | bytes 32768
  87.9 1.6 %copy.10 = bf16[2,3,256,64]{2,3,1,0:T(8,128)(2,1)} copy(bf16[2,3,256,64]{2,3,1,0:T(8,128)(2,1)} %bitcast.3) | data formatting | bytes 393216
